TPU v7x, 128 devices: a whole 4x4x4 slice. The times are simulated.
128 devices in a mesh: ty: 4 (over z_lo, core), tx: 32 (over y, x, z_hi).
Axes of the slice: x: 4, y: 4, z: 4 (z_hi: 2, z_lo: 2; z = z_hi * 2 + z_lo), core: 2. Of those that a mesh axis runs over, the one named last changes fastest.
Arguments:
- out_grad: bfloat16 [2, 128, 512, 192], P(None, 'ty', 'tx'), may hold values from -6 to 6
- preact: bfloat16 [2, 64, 256, 384], P(None, 'ty', 'tx'), may hold values from -8 to 8
- norm_gain: float32 [384], replicated, may hold values from 0.5 to 2
- mid_weight: bfloat16 [3, 3, 3, 384, 384], replicated, may hold values from -0.0625 to 0.0625
- up_weight: bfloat16 [3, 3, 3, 384, 192], replicated, may hold values from -0.078125 to 0.078125
- patch_weight: bfloat16 [3072, 2560], P(None, 'ty'), may hold values from -0.109375 to 0.109375
- query_proj: bfloat16 [4096, 2560], P('tx', 'ty'), may hold values from -4.6 to 4.6
- key_proj: bfloat16 [4096, 2560], P('tx', 'ty'), may hold values from -4.6 to 4.6
- value_proj: bfloat16 [4096, 2560], P('tx', 'ty'), may hold values from -6 to 6
- qkv_weight: bfloat16 [5120, 3, 2560], P('tx', None, 'ty'), may hold values from -0.0625 to 0.0625
Outputs:
- feature_grad: bfloat16 [2, 64, 256, 384], P(None, 'ty', 'tx')
- latent_grad: bfloat16 [4096, 5120], P('tx', 'ty')
All inputs are finite; a program needn't handle non-finite values.
Results may differ from a plain program's by a relative error of at most 0.03.
Values may be sent and summed in bfloat16 or wider, within the bound.
A program may use at most 192 MiB of HBM per device.

v0:
```python
import jax
import jax.numpy as jnp
from jax import lax
from jax.sharding import PartitionSpec as P

HEAD_DIM = 128


def padded_2(cells, sides, width):
    for axis, dim in sides:
        count = lax.axis_size(axis)
        ends = count - 1
        head = lax.slice_in_dim(cells, 0, width, axis=dim)
        tail = lax.slice_in_dim(cells, cells.shape[dim] - width, cells.shape[dim], axis=dim)
        cells = jnp.concatenate(
            [
                lax.ppermute(tail, axis, [(i, (i + 1) % count) for i in range(ends)]),
                cells,
                lax.ppermute(head, axis, [((i + 1) % count, i) for i in range(ends)]),
            ],
            axis=dim,
        )
    return cells


def transpose_conv(padded, weight):
    frames = padded.shape[0]
    out_rows = padded.shape[1] - 2
    out_cols = padded.shape[2] - 2
    extended = jnp.pad(padded, ((0, 2), (0, 0), (0, 0), (0, 0)))
    summed = jnp.zeros((frames, out_rows, out_cols, weight.shape[3]), jnp.float32)
    for tap_time in range(3):
        for tap_row in range(3):
            for tap_col in range(3):
                portion = extended[
                    2 - tap_time : 2 - tap_time + frames,
                    2 - tap_row : 2 - tap_row + out_rows,
                    2 - tap_col : 2 - tap_col + out_cols,
                ]
                summed = summed + lax.dot_general(
                    portion,
                    weight[tap_time, tap_row, tap_col],
                    (((3,), (1,)), ((), ())),
                    preferred_element_type=jnp.float32,
                )
    return summed


def pool_pairs(grid):
    frames, rows, cols, chans = grid.shape
    return grid.reshape(frames, rows // 2, 2, cols // 2, 2, chans).sum(axis=(2, 4))


def scale_back(pooled, preact, norm_gain):
    scaled = norm_gain * preact.astype(jnp.float32)
    sigmoid_val = jax.nn.sigmoid(scaled)
    return (pooled * norm_gain * sigmoid_val * (1.0 + scaled * (1.0 - sigmoid_val))).astype(
        jnp.bfloat16
    )


def body(
    out_grad,
    preact,
    norm_gain,
    mid_weight,
    up_weight,
    patch_weight,
    query_proj,
    key_proj,
    value_proj,
    qkv_weight,
):
    fine_pad = padded_2(out_grad, (("ty", 1), ("tx", 2)), 1)
    pooled = pool_pairs(transpose_conv(fine_pad, up_weight))
    mid_grad = scale_back(pooled, preact, norm_gain)
    mid_pad = padded_2(mid_grad, (("ty", 1), ("tx", 2)), 1)
    feature_grad = transpose_conv(mid_pad, mid_weight).astype(jnp.bfloat16)
    frame_count, tile_rows, tile_cols, channels = feature_grad.shape
    patches = feature_grad.reshape(frame_count, tile_rows // 2, 2, tile_cols // 2, 2, channels)
    patches = patches.transpose(1, 3, 0, 2, 4, 5).reshape(
        tile_rows // 2 * (tile_cols // 2), frame_count * 4 * channels
    )
    grad_out = jnp.dot(
        lax.all_gather(patches, "ty", axis=0, tiled=True),
        patch_weight,
        preferred_element_type=jnp.float32,
    ).astype(jnp.bfloat16)
    tok_count, head_cols = query_proj.shape
    heads_here = head_cols // HEAD_DIM
    score_factor = HEAD_DIM ** (-0.5)
    key_all, value_all = (
        lax.all_gather(key_proj, "tx", axis=0, tiled=True),
        lax.all_gather(value_proj, "tx", axis=0, tiled=True),
    )
    query_h = query_proj.reshape(tok_count, heads_here, HEAD_DIM)
    grad_h = grad_out.reshape(tok_count, heads_here, HEAD_DIM)
    key_h = key_all.reshape(-1, heads_here, HEAD_DIM)
    value_h = value_all.reshape(-1, heads_here, HEAD_DIM)
    scores = score_factor * jnp.einsum(
        "qhd,khd->hqk", query_h, key_h, preferred_element_type=jnp.float32
    )
    peak = jnp.max(scores, axis=-1, keepdims=True)
    expd = jnp.exp(scores - peak)
    totals = jnp.sum(expd, axis=-1, keepdims=True)
    probs = expd / totals
    probs_low = probs.astype(jnp.bfloat16)
    attended = jnp.einsum("hqk,khd->qhd", probs_low, value_h, preferred_element_type=jnp.float32)
    row_dot = jnp.sum(grad_h.astype(jnp.float32) * attended, axis=-1)
    grad_probs = jnp.einsum("qhd,khd->hqk", grad_h, value_h, preferred_element_type=jnp.float32)
    grad_low = (probs * (grad_probs - row_dot.T[:, :, None])).astype(jnp.bfloat16)
    grad_query = score_factor * jnp.einsum(
        "hqk,khd->qhd", grad_low, key_h, preferred_element_type=jnp.float32
    )
    key_term = score_factor * jnp.einsum(
        "hqk,qhd->khd", grad_low, query_h, preferred_element_type=jnp.float32
    )
    value_term = jnp.einsum("hqk,qhd->khd", probs_low, grad_h, preferred_element_type=jnp.float32)
    grad_key, grad_value = (
        lax.psum_scatter(
            key_term.reshape(-1, head_cols).astype(jnp.bfloat16),
            "tx",
            scatter_dimension=0,
            tiled=True,
        ).astype(jnp.float32),
        lax.psum_scatter(
            value_term.reshape(-1, head_cols).astype(jnp.bfloat16),
            "tx",
            scatter_dimension=0,
            tiled=True,
        ).astype(jnp.float32),
    )
    qkv_grad = jnp.stack(
        [grad_query.reshape(tok_count, head_cols), grad_key, grad_value], axis=1
    ).astype(jnp.bfloat16)
    head_part = lax.dot_general(
        qkv_grad,
        lax.all_gather(qkv_weight, "tx", axis=0, tiled=True),
        (((1, 2), (1, 2)), ((), ())),
        preferred_element_type=jnp.float32,
    )
    latent_grad = lax.psum_scatter(
        head_part.astype(jnp.bfloat16), "ty", scatter_dimension=1, tiled=True
    )
    return (feature_grad, latent_grad)


def solution(mesh):
    placed = (
        P(None, "ty", "tx", None),
        P(None, "ty", "tx", None),
        P(),
        P(),
        P(),
        P(None, "ty"),
        P("tx", "ty"),
        P("tx", "ty"),
        P("tx", "ty"),
        P("tx", None, "ty"),
    )
    return jax.shard_map(
        body,
        mesh=mesh,
        in_specs=placed,
        out_specs=(P(None, "ty", "tx", None), P("tx", "ty")),
        check_vma=False,
    )
```

profile of v0, /device:TPU:1, one launch (start us, length us, event | category | flops | bytes accessed | tf_op | source)
XLA Modules:
  0.0 858.5 jit_solution(11225905530886345406)
XLA Ops:
  7.2 1.7 copy.23
  9.7 4.9 collective-permute-start
  14.7 1.9 collective-permute-start.1
  16.6 1.7 copy.28
  18.4 2.6 fusion.143
  21.0 2.5 fusion.145
  23.5 2.5 fusion.147
  26.0 2.5 fusion.149
  28.5 2.6 fusion.151
  31.0 2.5 fusion.153
  33.5 2.5 fusion.155
  36.0 2.5 fusion.157
  38.5 2.5 fusion.159
  41.0 1.3 fusion.186
  44.8 1.3 convolution_add_fusion.17
  46.1 1.3 convolution_add_fusion.16
  54.1 5.5 collective-permute-start.2
  59.6 1.5 collective-permute-start.3
  61.0 1.3 fusion.34
  62.4 1.3 fusion.38
  63.7 2.4 collective-permute-done.3
  68.4 1.6 fusion.66
  70.0 1.6 fusion.68
  71.6 1.6 fusion.70
  73.3 1.6 fusion.72
  74.9 1.6 fusion.43
  76.5 1.6 fusion.46
  78.1 1.6 fusion.49
  79.7 1.6 fusion.52
  81.3 1.6 fusion.56
  82.9 1.6 fusion.74
  84.5 11.8 %add_add_fusion = f32[2,32,16,384]{3,2,1,0:T(8,128)} fusion(f32[2,32,16,384]{3,2,1,0:T(8,128)S(1)} %fusion.38, f32[2,32,16,384]{3,2,1,0:T(8,128)} %fusion.56, f32[2,32,16,384]{3,2,1,0:T(8,128)} %fusion.43, f32[2,32,16,384]{3,2,1,0:T(8,128)S(1)} %fusion.186, f32[2,32,16,384]{3,2,1,0:T(8,128)} %fusion.49, f32[2,32,16,384]{3,2,1,0:T(8,128)} %fusion.46, ...), kind=kOutput, calls=%fused_computation.24 | convolution fusion | flops 162004992 | bytes 43058688 | tf_op jit(solution)/shard_map/dot_general | solution.py:40
  96.3 2.3 reshape.33
  99.9 4.5 collective-permute-start.4
  104.4 1.9 collective-permute-start.5
  106.3 1.3 fusion.88
  107.6 2.2 collective-permute-done.5
  109.9 4.6 collective-permute-start.6
  114.5 1.5 collective-permute-start.7
  116.0 1.3 fusion.94
  117.3 1.3 fusion.83
  118.5 2.4 collective-permute-done.7
  135.3 1.3 convolution_add_fusion.3
  136.5 1.3 convolution_add_fusion.2
  137.8 1.3 fusion.20
  139.1 1.3 fusion.25
  140.7 8.1 all_gather.13
  148.8 2.9 convolution_convert_fusion.1
  151.9 10.0 %fusion.279 = (f32[5,128]{1,0:T(8,128)S(1)}, f32[5,128,4096]{2,1,0:T(8,128)}) fusion(bf16[128,5,128]{0,2,1:T(8,128)(2,1)S(1)} %bitcast.434, bf16[4096,5,128]{0,2,1:T(8,128)(2,1)} %bitcast.432), kind=kOutput, calls=%fused_computation.324 | convolution fusion | flops 678957056 | bytes 15895040 | tf_op jit(solution)/shard_map/sub | solution.py:104
  162.0 7.9 fusion.6
  169.9 64.9 %all-gather.6.cloned.1.call-done = bf16[4096,640]{0,1:T(8,128)(2,1)} async-done(((bf16[128,640]{0,1:T(8,128)(2,1)}), bf16[4096,640]{0,1:T(8,128)(2,1)}) %all-gather.6.cloned.1.call-update) | async-done | bytes 5242896 | tf_op jit(solution)/shard_map/all_gather | solution.py:94
  234.7 5.7 fusion.27
  240.5 1.3 copy-done
  241.8 4.7 multiply_convert_fusion.1
  246.4 4.1 multiply_convert_fusion
  250.5 7.8 copy.31
  258.7 6.3 convolution_convert_fusion
  265.0 7.8 copy.32
  273.5 5.6 fusion.26
  279.3 151.0 %reduce-scatter.4.cloned.1.call-done = bf16[128,640]{1,0:T(8,128)(2,1)} async-done(((bf16[4096,640]{1,0:T(8,128)(2,1)}), bf16[128,640]{1,0:T(8,128)(2,1)}) %reduce-scatter.4.cloned.1.call-update) | async-done | bytes 163856 | tf_op jit(solution)/shard_map/reduce_scatter | solution.py:120
  430.3 192.9 %reduce-scatter.6.cloned.1.call-done = bf16[128,640]{1,0:T(8,128)(2,1)} async-done(((bf16[4096,640]{1,0:T(8,128)(2,1)}), bf16[128,640]{1,0:T(8,128)(2,1)}) %reduce-scatter.6.cloned.1.call-update) | async-done | bytes 163856 | tf_op jit(solution)/shard_map/reduce_scatter | solution.py:126
  623.2 196.3 %all-gather.8.cloned.1.call-done = bf16[5120,3,640]{2,0,1:T(8,128)(2,1)} async-done(((bf16[160,3,640]{2,0,1:T(8,128)(2,1)}), bf16[5120,3,640]{2,0,1:T(8,128)(2,1)}) %all-gather.8.cloned.1.call-update) | async-done | bytes 19660816 | tf_op jit(solution)/shard_map/all_gather | solution.py:138
  819.5 11.3 %fusion.4 = bf16[128,5120]{1,0:T(8,128)(2,1)} fusion(bf16[5120,3,640]{2,0,1:T(8,128)(2,1)} %all-gather.8.cloned.1.call-done, bf16[128,1,640]{2,0,1:T(8,128)(2,1)} %bitcast.441, bf16[128,1,640]{2,0,1:T(8,128)(2,1)} %bitcast.440, bf16[128,1,640]{2,0,1:T(8,128)(2,1)S(1)} %copy.33), kind=kOutput, calls=%fused_computation.8 | convolution fusion | flops 2517729280 | bytes 21463040 | tf_op jit(solution)/shard_map/dot_general | solution.py:136
  830.8 20.4 %reduce-scatter.8.cloned.1.call-done = bf16[128,1280]{1,0:T(8,128)(2,1)} async-done(((bf16[128,5120]{1,0:T(8,128)(2,1)}), bf16[128,1280]{1,0:T(8,128)(2,1)}) %reduce-scatter.8.cloned.1.call-update) | async-done | bytes 327696 | tf_op jit(solution)/shard_map/reduce_scatter | solution.py:142
  (73 shorter events, 29.6 us)
Async XLA Ops:
  7.2 144.8 %all-gather.4.cloned.1.call-start = ((), (), s32[]{:S(2)}) async-start(), calls=%async_computation.3 | async-start | bytes 5406720 | tf_op jit(solution)/shard_map/all_gather | solution.py:93
  9.0 225.8 %all-gather.6.cloned.1.call-start = ((), (), s32[]{:S(2)}) async-start(), calls=%async_computation.4 | async-start | bytes 5406720 | tf_op jit(solution)/shard_map/all_gather | solution.py:94
  9.7 44.1 %collective-permute-start = (bf16[2,1,16,192]{3,2,1,0:T(8,128)(2,1)S(1)}, bf16[2,1,16,192]{3,2,1,0:T(8,128)(2,1)S(1)}, u32[]{:S(2)}, u32[]{:S(2)}) collective-permute-start(bf16[2,1,16,192]{3,2,1,0:T(8,128)(2,1)S(1)} %get-tuple-element.5), channel_id=1, source_target_pairs={{0,32},{32,64},{64,96},{1,33},{33,65},{65,97},{2,34},{34,66},{66,9... | collective-permute-start | bytes 36872 | tf_op jit(solution)/shard_map/ppermute | solution.py:17
  14.7 39.3 %collective-permute-start.1 = (bf16[2,1,16,192]{3,2,1,0:T(8,128)(2,1)S(1)}, bf16[2,1,16,192]{3,2,1,0:T(8,128)(2,1)S(1)}, u32[]{:S(2)}, u32[]{:S(2)}) collective-permute-start(bf16[2,1,16,192]{3,2,1,0:T(8,128)(2,1)S(1)} %get-tuple-element.4), channel_id=1, source_target_pairs={{32,0},{64,32},{96,64},{33,1},{65,33},{97,65},{34,2},{66,34},{98,6... | collective-permute-start | bytes 36872 | tf_op jit(solution)/shard_map/ppermute | solution.py:19
  18.3 412.0 %reduce-scatter.4.cloned.1.call-start = ((), (), s32[]{:S(2)}) async-start(), calls=%async_computation.5 | async-start | bytes 5406720 | tf_op jit(solution)/shard_map/reduce_scatter | solution.py:120
  28.5 12.5 %copy-start.2 = (bf16[2,32,16,192]{3,2,1,0:T(8,128)(2,1)S(1)}, bf16[2,32,16,192]{3,2,1,0:T(8,128)(2,1)}, u32[]{:S(2)}) copy-start(bf16[2,32,16,192]{3,2,1,0:T(8,128)(2,1)} %param.10) | copy-start | bytes 1179652
  44.8 8.9 %copy-start.6 = (bf16[128,640]{1,0:T(8,128)(2,1)S(1)}, bf16[128,640]{1,0:T(8,128)(2,1)}, u32[]{:S(2)}) copy-start(bf16[128,640]{1,0:T(8,128)(2,1)} %param.16) | copy-start | bytes 491524
  53.9 12.8 %copy-start.3 = (bf16[3,3,3,384,192]{3,4,2,1,0:T(8,128)(2,1)S(1)}, bf16[3,3,3,384,192]{3,4,2,1,0:T(8,128)(2,1)}, u32[]{:S(2)}) copy-start(bf16[3,3,3,384,192]{3,4,2,1,0:T(8,128)(2,1)} %param.14) | copy-start | bytes 11943940
  54.1 9.6 %collective-permute-start.2 = (bf16[2,34,1,192]{3,2,1,0:T(2,128)(2,1)S(1)}, bf16[2,34,1,192]{3,2,1,0:T(2,128)(2,1)S(1)}, u32[]{:S(2)}, u32[]{:S(2)}) collective-permute-start(bf16[2,34,1,192]{3,2,1,0:T(2,128)(2,1)S(1)} %get-tuple-element.2), channel_id=1, source_target_pairs={{0,1},{1,2},{2,3},{3,4},{4,5},{5,6},{6,7},{7,8},{8,9},{9,10},{10,1... | collective-permute-start | bytes 78344 | tf_op jit(solution)/shard_map/ppermute | solution.py:17
  59.6 6.6 collective-permute-start.3
  96.3 3.4 copy-start.5
  96.3 3.4 copy-start.7
  99.9 7.7 collective-permute-start.4
  104.4 5.4 collective-permute-start.5
  109.9 8.6 %collective-permute-start.6 = (bf16[2,18,1,384]{3,2,1,0:T(2,128)(2,1)S(1)}, bf16[2,18,1,384]{3,2,1,0:T(2,128)(2,1)S(1)}, u32[]{:S(2)}, u32[]{:S(2)}) collective-permute-start(bf16[2,18,1,384]{3,2,1,0:T(2,128)(2,1)S(1)} %get-tuple-element.9), channel_id=1, source_target_pairs={{0,1},{1,2},{2,3},{3,4},{4,5},{5,6},{6,7},{7,8},{8,9},{9,10},{10,1... | collective-permute-start | bytes 82952 | tf_op jit(solution)/shard_map/ppermute | solution.py:17
  114.5 6.4 collective-permute-start.7
  140.4 21.6 %copy-start.4 = (bf16[2,16,8,384]{3,2,1,0:T(8,128)(2,1)}, bf16[2,16,8,384]{3,2,1,0:T(8,128)(2,1)S(1)}, u32[]{:S(2)}) copy-start(bf16[2,16,8,384]{3,2,1,0:T(8,128)(2,1)S(1)} %fusion.25) | copy-start | bytes 589828
  234.7 7.0 copy-start
  246.4 4.1 copy-start.1
  258.4 364.8 %reduce-scatter.6.cloned.1.call-start = ((), (), s32[]{:S(2)}) async-start(), calls=%async_computation.6 | async-start | bytes 5406720 | tf_op jit(solution)/shard_map/reduce_scatter | solution.py:126
  272.9 546.6 %all-gather.8.cloned.1.call-start = ((), (), s32[]{:S(2)}) async-start(), calls=%async_computation.7 | async-start | bytes 20275200 | tf_op jit(solution)/shard_map/all_gather | solution.py:138
  273.5 577.8 %reduce-scatter.8.cloned.1.call-start = ((), (), s32[]{:S(2)}) async-start(), calls=%async_computation.8 | async-start | bytes 1638400 | tf_op jit(solution)/shard_map/reduce_scatter | solution.py:142
Sparse Core Ops, SparseCore 0:
  11.3 112.4 all-gather.3
  126.6 108.0 all-gather.5
  258.5 171.7 reduce-scatter.3
  432.6 190.5 reduce-scatter.5
  626.1 193.3 all-gather.7
  831.0 20.2 reduce-scatter.7
where the time goes:
time: 865 us; the launch traced here: 859 us
  waiting for transfers between devices  633 us (73%)
  matrix products  141 us (16%)
  starting transfers between devices  26.8 us (3%)
  local copies, waits for them, and re-layouts  24.5 us (3%)
  between operations  15.1 us (2%)
  other arithmetic  10.4 us (1%)
    all_gather x1, waiting for transfers between devices, body(): lax.all_gather(qkv_weight, 'tx', axis=0, tiled=True)  196 us
    reduce_scatter x1, waiting for transfers between devices, body(): lax.psum_scatter(value_term.reshape(-1, head_cols).astype(jnp.bfloat16),...  193 us
    reduce_scatter x1, waiting for transfers between devices, body(): lax.psum_scatter(key_term.reshape(-1, head_cols).astype(jnp.bfloat16), 't...  151 us
    dot_general x54, matrix products, transpose_conv(): lax.dot_general(portion, weight[tap_time, tap_row, tap_col], (((3,), (1,)...  90 us
    all_gather x1, waiting for transfers between devices, body(): lax.all_gather(value_proj, 'tx', axis=0, tiled=True)  64.9 us
    reduce_scatter x1, waiting for transfers between devices, body(): lax.psum_scatter(head_part.astype(jnp.bfloat16), 'ty', scatter_dimension=...  20.4 us
    ppermute x4, starting transfers between devices, padded_2(): lax.ppermute(tail, axis, [(i, (i + 1) % count) for i in range(ends)])  19.4 us
  transfers between devices with their start and end apart: 14, of which 8 were waited for; matrix products, arithmetic and copies ran while one was open for 16% of the time, Pallas kernels for 0%

commit v1 on v0

v1 whole, which is shorter than its diff:
```python
import jax
import jax.numpy as jnp
from jax import lax
from jax.sharding import Mesh
from jax.sharding import PartitionSpec as P

HEAD_DIM = 128


def padded(cells, sides, width):
    for axis, dim in sides:
        count = lax.axis_size(axis)
        ends = count - 1
        head = lax.slice_in_dim(cells, 0, width, axis=dim)
        tail = lax.slice_in_dim(cells, cells.shape[dim] - width, cells.shape[dim], axis=dim)
        cells = jnp.concatenate(
            [
                lax.ppermute(tail, axis, [(i, (i + 1) % count) for i in range(ends)]),
                cells,
                lax.ppermute(head, axis, [((i + 1) % count, i) for i in range(ends)]),
            ],
            axis=dim,
        )
    return cells


def conv(cells, weight, stride):
    return lax.conv_general_dilated(
        cells,
        lax.rev(weight, (0, 1)),
        (stride, stride),
        "VALID",
        dimension_numbers=("NHWC", "HWOI", "NHWC"),
        preferred_element_type=jnp.float32,
    )


def causal(cells, weight, stride):
    own = conv(cells, weight[2], stride)
    later = conv(cells[1:], weight[1], stride)
    return own + jnp.pad(later, ((0, 1), (0, 0), (0, 0), (0, 0)))


def scale_back(pooled, preact, norm_gain):
    scaled = norm_gain * preact.astype(jnp.float32)
    sigmoid_val = jax.nn.sigmoid(scaled)
    return (pooled * norm_gain * sigmoid_val * (1.0 + scaled * (1.0 - sigmoid_val))).astype(
        jnp.bfloat16
    )


def body(
    out_grad,
    preact,
    norm_gain,
    mid_weight,
    up_weight,
    patch_weight,
    query_proj,
    key_proj,
    value_proj,
    qkv_weight,
):
    bf = jnp.bfloat16
    f32 = jnp.float32
    w_all = lax.all_gather(qkv_weight, "m", axis=0, tiled=True)
    key_all = lax.all_gather(key_proj, "y", axis=0, tiled=True)
    value_all = lax.all_gather(value_proj, "y", axis=0, tiled=True)
    query_all = lax.all_gather(query_proj, "m", axis=0, tiled=True)
    fine = padded(out_grad, (("ty", 1), (("y", "m"), 2)), 1).astype(f32)
    fine = fine[:, :-1] + fine[:, 1:]
    fine = (fine[:, :, :-1] + fine[:, :, 1:]).astype(bf)
    pooled = causal(fine, up_weight, 2)
    mid_grad = scale_back(pooled, preact, norm_gain)
    mid_pad = padded(mid_grad, (("ty", 1), (("y", "m"), 2)), 1)
    feature_grad = causal(mid_pad, mid_weight, 1).astype(bf)
    frame_count, tile_rows, tile_cols, channels = feature_grad.shape
    patches = feature_grad.reshape(frame_count, tile_rows // 2, 2, tile_cols // 2, 2, channels)
    patches = patches.transpose(1, 3, 0, 2, 4, 5).reshape(
        tile_rows // 2 * (tile_cols // 2), frame_count * 4 * channels
    )
    grad_out = jnp.dot(
        lax.all_gather(patches, "ty", axis=0, tiled=True),
        patch_weight,
        preferred_element_type=f32,
    ).astype(bf)
    tok_count, head_cols = query_proj.shape
    heads = head_cols // HEAD_DIM
    factor = HEAD_DIM ** (-0.5)

    def split(rows):
        return rows.reshape(-1, heads, HEAD_DIM)

    def dots(spec, one, two):
        return jnp.einsum(spec, one, two, preferred_element_type=f32)

    query_h, key_h, value_h = split(query_all), split(key_all), split(value_all)
    scores = factor * dots("qhd,khd->hqk", query_h, key_h)
    peak = lax.pmax(jnp.max(scores, axis=-1, keepdims=True), "m")
    expd = jnp.exp(scores - peak)
    totals = lax.psum(jnp.sum(expd, axis=-1, keepdims=True), "m")
    probs = expd / totals
    probs_low = probs.astype(bf)
    grad_h = split(lax.all_gather(grad_out, "m", axis=0, tiled=True))
    grad_probs = dots("qhd,khd->hqk", grad_h, value_h)
    row_dot = lax.psum(jnp.sum(probs * grad_probs, axis=-1, keepdims=True), "m")
    grad_low = (probs * (grad_probs - row_dot)).astype(bf)
    grad_query = factor * dots("hqk,khd->qhd", grad_low, key_h)
    grad_key = factor * dots("hqk,qhd->khd", grad_low, query_h)
    grad_value = dots("hqk,qhd->khd", probs_low, grad_h)

    def scatter(rows, axis):
        rows = rows.reshape(-1, head_cols).astype(bf)
        return lax.psum_scatter(rows, axis, scatter_dimension=0, tiled=True)

    qkv_grad = jnp.stack(
        [scatter(grad_query, "m"), scatter(grad_key, "y"), scatter(grad_value, "y")], axis=1
    )
    head_part = lax.dot_general(
        lax.all_gather(qkv_grad, "y", axis=0, tiled=True),
        w_all,
        (((1, 2), (1, 2)), ((), ())),
        preferred_element_type=f32,
    )
    part = lax.psum_scatter(head_part.astype(bf), "ty", scatter_dimension=0, tiled=True)
    count = lax.axis_size("ty")
    latent_grad = lax.ppermute(
        part,
        ("ty", "y"),
        [(i * count + j, j * count + i) for i in range(count) for j in range(count)],
    )
    return (feature_grad, latent_grad)


def solution(mesh):
    rows, cols = mesh.devices.shape
    split = Mesh(mesh.devices.reshape(rows, rows, cols // rows), ("ty", "y", "m"))
    tx = ("y", "m")
    placed = (
        P(None, "ty", tx, None),
        P(None, "ty", tx, None),
        P(),
        P(),
        P(),
        P(None, "ty"),
        P(tx, "ty"),
        P(tx, "ty"),
        P(tx, "ty"),
        P(tx, None, "ty"),
    )
    return jax.shard_map(
        body,
        mesh=split,
        in_specs=placed,
        out_specs=(P(None, "ty", tx, None), P(tx, "ty")),
        check_vma=False,
    )
```

time: 865 us -> 523 us (0.60)
  waiting for transfers between devices: 633 us -> 250 us
  blocking collectives: 8.08 us -> 141 us
  matrix products: 141 us -> 49.5 us
  local copies, waits for them, and re-layouts: 24.5 us -> 13.6 us
    reduce_scatter x3 -> x4, waiting for transfers between devices: 364 us -> 132 us  [the longest x3 111 us: scatter(): return lax.psum_scatter(rows, axis, scatter_dimension=0, tiled=True)]
    all_gather x3 -> x4, waiting for transfers between devices: 261 us -> 109 us  [the longest x1 79.7 us: body(): w_all = lax.all_gather(qkv_weight, 'm', axis=0, tiled=True)]
    dot_general x60 -> x6, matrix products: 128 us -> 33.5 us  [the longest x5 26.5 us: dots(): return jnp.einsum(spec, one, two, preferred_element_type=f32)]
    psum x0 -> x2, blocking collectives: none -> 60.4 us  [the longest x1 30.5 us: body(): row_dot = lax.psum(jnp.sum(probs * grad_probs, axis=-1, keepdims=True), 'm')]
    all_gather x0 -> x2, blocking collectives: none -> 36 us  [the longest x1 22 us: body(): key_all = lax.all_gather(key_proj, 'y', axis=0, tiled=True)]
    pmax x0 -> x1, blocking collectives: none -> 30.5 us  [body(): peak = lax.pmax(jnp.max(scores, axis=-1, keepdims=True), 'm')]
    conv_general_dilated x0 -> x4, matrix products: none -> 12.4 us  [conv(): lax.conv_general_dilated(cells, lax.rev(weight, (0, 1)), (stride, stride)...]
    convert_element_type x3 -> x4, local copies, waits for them, and re-layouts: 15.8 us -> 3.86 us  [the longest x3 3.66 us: scatter(): rows = rows.reshape(-1, head_cols).astype(bf)]
  transfers between devices with their start and end apart: 14 -> 17, of which waited for: 8 -> 9; matrix products, arithmetic and copies ran while one was open for 16% -> 12% of each run, Pallas kernels for 0% -> 0%
where the time goes in v1:
time: 523 us; the launch traced here: 518 us
  waiting for transfers between devices  250 us (48%)
  blocking collectives  141 us (27%)
  matrix products  49.5 us (9%)
  starting transfers between devices  31.2 us (6%)
  other arithmetic  17.7 us (3%)
  between operations  14.6 us (3%)
  local copies, waits for them, and re-layouts  13.6 us (3%)
    reduce_scatter x3, waiting for transfers between devices, scatter(): return lax.psum_scatter(rows, axis, scatter_dimension=0, tiled=True)  111 us
    all_gather x1, waiting for transfers between devices, body(): w_all = lax.all_gather(qkv_weight, 'm', axis=0, tiled=True)  79.7 us
    psum x1, blocking collectives, body(): row_dot = lax.psum(jnp.sum(probs * grad_probs, axis=-1, keepdims=True), 'm')  30.5 us
    pmax x1, blocking collectives, body(): peak = lax.pmax(jnp.max(scores, axis=-1, keepdims=True), 'm')  30.5 us
    psum x1, blocking collectives, body(): totals = lax.psum(jnp.sum(expd, axis=-1, keepdims=True), 'm')  29.8 us
    all_gather x1, waiting for transfers between devices, body(): lax.all_gather(qkv_grad, 'y', axis=0, tiled=True)  29.4 us
    dot_general x5, matrix products, dots(): return jnp.einsum(spec, one, two, preferred_element_type=f32)  26.5 us
    all_gather x1, blocking collectives, body(): key_all = lax.all_gather(key_proj, 'y', axis=0, tiled=True)  22 us
  transfers between devices with their start and end apart: 17, of which 9 were waited for; matrix products, arithmetic and copies ran while one was open for 12% of the time, Pallas kernels for 0%

profile of v1, /device:TPU:1, one launch (start us, length us, event | category | flops | bytes accessed | tf_op | source)
XLA Modules:
  0.0 517.9 jit_solution(11201211064460353302)
XLA Ops:
  7.2 0.7 fusion.67
  8.0 4.9 collective-permute-start
  12.9 1.9 collective-permute-start.1
  14.8 1.1 constant_dynamic-update-slice_fusion.1
  15.9 2.0 collective-permute-done.1
  18.1 1.3 collective-permute-start.3
  19.4 5.8 %collective-permute-start.2 = (bf16[2,34,1,192]{3,2,1,0:T(2,128)(2,1)S(1)}, bf16[2,34,1,192]{3,2,1,0:T(2,128)(2,1)S(1)}, u32[]{:S(2)}, u32[]{:S(2)}) collective-permute-start(bf16[2,34,1,192]{3,2,1,0:T(2,128)(2,1)S(1)} %get-tuple-element.8), channel_id=1, source_target_pairs={{0,1},{1,2},{2,3},{3,4},{4,5},{5,6},{6,7},{7,8},{8,9},{9,10},{10,1... | collective-permute-start | bytes 78344 | tf_op jit(solution)/shard_map/ppermute | solution.py:18
  25.2 1.7 copy.61
  27.0 0.4 maximum_convert_fusion
  27.5 0.2 fusion.82
  27.8 0.2 fusion.18
  28.0 0.2 pad.9
  28.3 0.4 reshape.40
  28.6 0.2 copy.52
  28.8 0.1 slice.82
  29.0 2.5 fusion.30
  31.5 0.5 copy.53
  32.1 0.2 reshape.45
  32.6 2.0 fusion.35
  34.9 0.2 fusion.56
  35.2 1.9 collective-permute-start.5
  37.1 3.6 collective-permute-start.4
  40.7 0.8 collective-permute-done.4
  41.6 1.3 collective-permute-start.7
  42.9 6.4 %collective-permute-start.6 = (bf16[2,18,1,384]{3,2,1,0:T(2,128)(2,1)S(1)}, bf16[2,18,1,384]{3,2,1,0:T(2,128)(2,1)S(1)}, u32[]{:S(2)}, u32[]{:S(2)}) collective-permute-start(bf16[2,18,1,384]{3,2,1,0:T(2,128)(2,1)S(1)} %get-tuple-element.12), channel_id=1, source_target_pairs={{0,1},{1,2},{2,3},{3,4},{4,5},{5,6},{6,7},{7,8},{8,9},{9,10},{10,1... | collective-permute-start | bytes 82952 | tf_op jit(solution)/shard_map/ppermute | solution.py:18
  49.3 1.2 collective-permute-done.6
  50.6 0.3 pad_maximum_fusion.1
  50.8 3.9 fusion.6
  54.7 4.0 fusion.41
  58.7 0.2 copy.104
  59.0 14.2 %all_gather.23 = bf16[128,3072]{1,0:T(8,128)(2,1)S(1)} all-gather(bf16[32,3072]{1,0:T(8,128)(2,1)S(1)} %reshape.32), channel_id=1, replica_groups=mesh['ty'=4,'y'=4,'m'=8] {'ty'}, dimensions={0}, use_global_device_ids=true | all-gather | bytes 983040 | tf_op jit(solution)/shard_map/all_gather | solution.py:83
  73.2 3.6 convolution_convert_fusion
  76.9 0.2 copy.62
  77.1 0.2 copy.67
  77.3 22.0 %all_gather.22 = bf16[512,640]{0,1:T(8,128)(2,1)S(1)} all-gather(bf16[128,640]{0,1:T(8,128)(2,1)S(1)} %copy.62), channel_id=1, replica_groups=mesh['ty'=4,'y'=4,'m'=8] {'y'}, dimensions={0}, use_global_device_ids=true | all-gather | bytes 819200 | tf_op jit(solution)/shard_map/all_gather | solution.py:67
  99.2 14.0 %all_gather.25 = bf16[512,640]{0,1:T(8,128)(2,1)S(1)} all-gather(bf16[128,640]{0,1:T(8,128)(2,1)S(1)} %copy.67), channel_id=1, replica_groups=mesh['ty'=4,'y'=4,'m'=8] {'y'}, dimensions={0}, use_global_device_ids=true | all-gather | bytes 819200 | tf_op jit(solution)/shard_map/all_gather | solution.py:68
  113.3 6.9 %multiply_reduce_fusion.1 = (f32[5,1024]{1,0:T(8,128)S(1)}, f32[5,1024,512]{1,2,0:T(8,128)}) fusion(bf16[1024,5,128]{0,2,1:T(8,128)(2,1)} %bitcast.98, bf16[512,5,128]{0,2,1:T(8,128)(2,1)S(1)} %bitcast.95), kind=kOutput, calls=%fused_computation.3 | convolution fusion | flops 676326400 | bytes 12472320 | tf_op jit(solution)/shard_map/qhd,khd->hqk/dot_general | solution.py:95
  120.2 30.5 %pmax.7 = f32[5,1024]{1,0:T(8,128)S(1)} all-reduce(f32[5,1024]{1,0:T(8,128)S(1)} %get-tuple-element.16), channel_id=1, replica_groups=mesh['ty'=4,'y'=4,'m'=8] {'m'}, use_global_device_ids=true, to_apply=%region_1.2 | all-reduce | flops 5120 | bytes 40960 | tf_op jit(solution)/shard_map/pmax | solution.py:99
  150.7 5.7 %fusion.1 = f32[5,1024]{1,0:T(8,128)S(1)} fusion(f32[5,1024,512]{1,2,0:T(8,128)} %get-tuple-element.17, f32[5,1024]{1,0:T(8,128)S(1)} %pmax.7), kind=kLoop, calls=%fused_computation.5 | loop fusion | flops 7859200 | bytes 10526720 | tf_op jit(solution)/shard_map/reduce_sum | solution.py:101
  156.4 29.8 %psum.14 = f32[5,1024]{1,0:T(8,128)S(1)} all-reduce(f32[5,1024]{1,0:T(8,128)S(1)} %fusion.1), channel_id=1, replica_groups=mesh['ty'=4,'y'=4,'m'=8] {'m'}, use_global_device_ids=true, to_apply=%region_3.4 | all-reduce | flops 5120 | bytes 40960 | tf_op jit(solution)/shard_map/psum | solution.py:101
  186.2 1.6 copy.66
  187.8 6.4 %fusion.21 = bf16[5,128,512]{2,1,0:T(8,128)(2,1)S(1)} fusion(bf16[1024,5,128]{0,2,1:T(8,128)(2,1)S(1)} %bitcast.100, f32[5,1024,512]{1,2,0:T(8,128)} %get-tuple-element.17, f32[5,1024]{1,0:T(8,128)S(1)} %psum.14, f32[5,1024]{1,0:T(8,128)S(1)} %pmax.7), kind=kOutput, calls=%fused_computation.31 | convolution fusion | flops 681902080 | bytes 12492800 | tf_op jit(solution)/shard_map/hqk,qhd->khd/dot_general | solution.py:95
  194.2 1.1 copy.75
  195.3 8.0 %multiply_reduce_fusion = (f32[5,1024]{1,0:T(8,128)S(1)}, f32[5,1024,512]{1,2,0:T(8,128)}) fusion(f32[5,1024]{1,0:T(8,128)S(1)} %psum.14, f32[5,1024]{1,0:T(8,128)S(1)} %pmax.7, f32[5,1024,512]{1,2,0:T(8,128)} %get-tuple-element.17, bf16[1024,5,128]{0,2,1:T(8,128)(2,1)S(1)} %bitcast.101, bf16[512,5,128]{0,2,1:T(8,128)(2,1)S(1)} %bitcast.106), kind=kOutput, calls=%fused_computation.1 | convolution fusion | flops 684190720 | bytes 22999040 | tf_op jit(solution)/shard_map/qhd,khd->hqk/dot_general | solution.py:95
  203.4 30.5 %psum.15 = f32[5,1024]{1,0:T(8,128)S(1)} all-reduce(f32[5,1024]{1,0:T(8,128)S(1)} %get-tuple-element.18), channel_id=1, replica_groups=mesh['ty'=4,'y'=4,'m'=8] {'m'}, use_global_device_ids=true, to_apply=%region_5.6 | all-reduce | flops 5120 | bytes 40960 | tf_op jit(solution)/shard_map/psum | solution.py:106
  233.9 8.5 %multiply_convert_fusion = bf16[5,1024,512]{1,2,0:T(8,128)(2,1)S(1)} fusion(f32[5,1024,512]{1,2,0:T(8,128)} %get-tuple-element.19, f32[5,1024]{1,0:T(8,128)S(1)} %psum.15, f32[5,1024]{1,0:T(8,128)S(1)} %psum.14, f32[5,1024]{1,0:T(8,128)S(1)} %pmax.7, f32[5,1024,512]{1,2,0:T(8,128)} %get-tuple-element.17), kind=kLoop, calls=%fused_computation | loop fusion | flops 15728640 | bytes 26275840 | tf_op jit(solution)/shard_map/convert_element_type | solution.py:107
  242.4 1.9 fusion.24
  244.3 0.4 copy-done
  244.7 1.1 copy.73
  245.8 0.3 reduce-scatter.5.cloned.1.call-start
  246.1 3.4 multiply_convert_fusion.1
  249.5 1.5 copy.71
  251.0 34.5 %reduce-scatter.7.cloned.1.call-done = bf16[128,640]{1,0:T(8,128)(2,1)} async-done(((bf16[512,640]{1,0:T(8,128)(2,1)}), bf16[128,640]{1,0:T(8,128)(2,1)}) %reduce-scatter.7.cloned.1.call-update) | async-done | bytes 163856 | tf_op jit(solution)/shard_map/reduce_scatter | solution.py:114
  285.5 76.9 %reduce-scatter.5.cloned.1.call-done = bf16[128,640]{1,0:T(8,128)(2,1)} async-done(((bf16[1024,640]{1,0:T(8,128)(2,1)}), bf16[128,640]{1,0:T(8,128)(2,1)}) %reduce-scatter.5.cloned.1.call-update) | async-done | bytes 163856 | tf_op jit(solution)/shard_map/reduce_scatter | solution.py:114
  362.4 1.9 pad_maximum_fusion
  364.4 0.7 all-gather.11.cloned.1.call-update
  365.2 29.4 %all-gather.9.cloned.1.call-done = bf16[512,3,640]{2,0,1:T(8,128)(2,1)} async-done(((bf16[128,3,640]{2,0,1:T(8,128)(2,1)}), bf16[512,3,640]{2,0,1:T(8,128)(2,1)}) %all-gather.9.cloned.1.call-update) | async-done | bytes 1966096 | tf_op jit(solution)/shard_map/all_gather | solution.py:120
  394.6 79.7 %all-gather.11.cloned.1.call-done = bf16[1280,3,640]{2,0,1:T(8,128)(2,1)} async-done(((bf16[160,3,640]{2,0,1:T(8,128)(2,1)}), bf16[1280,3,640]{2,0,1:T(8,128)(2,1)}) %all-gather.11.cloned.1.call-update) | async-done | bytes 4915216 | tf_op jit(solution)/shard_map/all_gather | solution.py:66
  474.3 7.0 %fusion.5 = bf16[512,1280]{1,0:T(8,128)(2,1)} fusion(bf16[512,3,640]{2,0,1:T(8,128)(2,1)} %all-gather.9.cloned.1.call-done, bf16[1280,3,640]{2,0,1:T(8,128)(2,1)} %all-gather.11.cloned.1.call-done), kind=kOutput, calls=%fused_computation.11 | convolution fusion | flops 2517237760 | bytes 8192000 | tf_op jit(solution)/shard_map/dot_general | solution.py:119
  481.3 20.4 %reduce-scatter.11.cloned.1.call-done = bf16[128,1280]{1,0:T(8,128)(2,1)} async-done(((bf16[512,1280]{1,0:T(8,128)(2,1)}), bf16[128,1280]{1,0:T(8,128)(2,1)}) %reduce-scatter.11.cloned.1.call-update) | async-done | bytes 327696 | tf_op jit(solution)/shard_map/reduce_scatter | solution.py:125
  501.8 3.4 collective-permute-start.8
  505.2 0.7 copy.76
  505.9 4.5 collective-permute-done.8
  510.4 0.7 copy.108
  (53 shorter events, 1.6 us)
Async XLA Ops:
  7.2 106.1 %all-gather.5.cloned.1.call-start = ((), (), s32[]{:S(2)}) async-start(), calls=%async_computation.4 | async-start | bytes 1474560 | tf_op jit(solution)/shard_map/all_gather | solution.py:69
  8.0 6.9 %collective-permute-start = (bf16[2,1,16,192]{3,2,1,0:T(8,128)(2,1)S(1)}, bf16[2,1,16,192]{3,2,1,0:T(8,128)(2,1)S(1)}, u32[]{:S(2)}, u32[]{:S(2)}) collective-permute-start(bf16[2,1,16,192]{3,2,1,0:T(8,128)(2,1)S(1)} %get-tuple-element.11), channel_id=1, source_target_pairs={{0,32},{32,64},{64,96},{1,33},{33,65},{65,97},{2,34},{34,66},{66,9... | collective-permute-start | bytes 36872 | tf_op jit(solution)/shard_map/ppermute | solution.py:18
  12.9 5.1 collective-permute-start.1
  18.1 8.9 %collective-permute-start.3 = (bf16[2,34,1,192]{3,2,1,0:T(2,128)(2,1)S(1)}, bf16[2,34,1,192]{3,2,1,0:T(2,128)(2,1)S(1)}, u32[]{:S(2)}, u32[]{:S(2)}) collective-permute-start(bf16[2,34,1,192]{3,2,1,0:T(2,128)(2,1)S(1)} %get-tuple-element.9), channel_id=1, source_target_pairs={{1,0},{2,1},{3,2},{4,3},{5,4},{6,5},{7,6},{8,7},{9,8},{10,9},{11,1... | collective-permute-start | bytes 78344 | tf_op jit(solution)/shard_map/ppermute | solution.py:20
  19.4 7.7 %collective-permute-start.2 = (bf16[2,34,1,192]{3,2,1,0:T(2,128)(2,1)S(1)}, bf16[2,34,1,192]{3,2,1,0:T(2,128)(2,1)S(1)}, u32[]{:S(2)}, u32[]{:S(2)}) collective-permute-start(bf16[2,34,1,192]{3,2,1,0:T(2,128)(2,1)S(1)} %get-tuple-element.8), channel_id=1, source_target_pairs={{0,1},{1,2},{2,3},{3,4},{4,5},{5,6},{6,7},{7,8},{8,9},{9,10},{10,1... | collective-permute-start | bytes 78344 | tf_op jit(solution)/shard_map/ppermute | solution.py:18
  27.0 159.2 %all-gather.7.cloned.1.call-start = ((), (), s32[]{:S(2)}) async-start(), calls=%async_computation.5 | async-start | bytes 1474560 | tf_op jit(solution)/shard_map/all_gather | solution.py:104
  28.2 0.7 copy-start.7
  31.9 0.7 copy-start.6
  32.6 2.3 copy-start.2
  32.6 2.3 copy-start.5
  35.2 5.6 %collective-permute-start.5 = (bf16[2,1,8,384]{3,2,1,0:T(8,128)(2,1)S(1)}, bf16[2,1,8,384]{3,2,1,0:T(8,128)(2,1)S(1)}, u32[]{:S(2)}, u32[]{:S(2)}) collective-permute-start(bf16[2,1,8,384]{3,2,1,0:T(8,128)(2,1)S(1)} %get-tuple-element.15), channel_id=1, source_target_pairs={{32,0},{64,32},{96,64},{33,1},{65,33},{97,65},{34,2},{66,34},{98,6... | collective-permute-start | bytes 36872 | tf_op jit(solution)/shard_map/ppermute | solution.py:20
  37.1 4.5 collective-permute-start.4
  41.6 7.7 %collective-permute-start.7 = (bf16[2,18,1,384]{3,2,1,0:T(2,128)(2,1)S(1)}, bf16[2,18,1,384]{3,2,1,0:T(2,128)(2,1)S(1)}, u32[]{:S(2)}, u32[]{:S(2)}) collective-permute-start(bf16[2,18,1,384]{3,2,1,0:T(2,128)(2,1)S(1)} %get-tuple-element.13), channel_id=1, source_target_pairs={{1,0},{2,1},{3,2},{4,3},{5,4},{6,5},{7,6},{8,7},{9,8},{10,9},{11,1... | collective-permute-start | bytes 82952 | tf_op jit(solution)/shard_map/ppermute | solution.py:20
  42.9 7.6 %collective-permute-start.6 = (bf16[2,18,1,384]{3,2,1,0:T(2,128)(2,1)S(1)}, bf16[2,18,1,384]{3,2,1,0:T(2,128)(2,1)S(1)}, u32[]{:S(2)}, u32[]{:S(2)}) collective-permute-start(bf16[2,18,1,384]{3,2,1,0:T(2,128)(2,1)S(1)} %get-tuple-element.12), channel_id=1, source_target_pairs={{0,1},{1,2},{2,3},{3,4},{4,5},{5,6},{6,7},{7,8},{8,9},{9,10},{10,1... | collective-permute-start | bytes 82952 | tf_op jit(solution)/shard_map/ppermute | solution.py:18
  73.2 3.7 copy-start.3
  73.2 3.9 copy-start.4
  76.9 174.1 %reduce-scatter.9.cloned.1.call-start = ((), (), s32[]{:S(2)}) async-start(), calls=%async_computation.8 | async-start | bytes 819200 | tf_op jit(solution)/shard_map/reduce_scatter | solution.py:114
  195.3 90.3 %reduce-scatter.7.cloned.1.call-start = ((), (), s32[]{:S(2)}) async-start(), calls=%async_computation.7 | async-start | bytes 819200 | tf_op jit(solution)/shard_map/reduce_scatter | solution.py:114
  233.9 8.5 %copy-start.1 = (bf16[1024,640]{0,1:T(8,128)(2,1)S(1)}, bf16[1024,640]{0,1:T(8,128)(2,1)}, u32[]{:S(2)}) copy-start(bf16[1024,640]{0,1:T(8,128)(2,1)} %all-gather.5.cloned.1.call-done) | copy-start | bytes 3932164
  242.4 2.3 copy-start
  245.8 116.6 %reduce-scatter.5.cloned.1.call-start = ((), (), s32[]{:S(2)}) async-start(), calls=%async_computation.6 | async-start | bytes 1474560 | tf_op jit(solution)/shard_map/reduce_scatter | solution.py:114
  250.9 143.7 %all-gather.9.cloned.1.call-start = ((), (), s32[]{:S(2)}) async-start(), calls=%async_computation.9 | async-start | bytes 2457600 | tf_op jit(solution)/shard_map/all_gather | solution.py:120
  364.4 110.0 %all-gather.11.cloned.1.call-start = ((), (), s32[]{:S(2)}) async-start(), calls=%async_computation.10 | async-start | bytes 5529600 | tf_op jit(solution)/shard_map/all_gather | solution.py:66
  365.1 136.6 %reduce-scatter.11.cloned.1.call-start = ((), (), s32[]{:S(2)}) async-start(), calls=%async_computation.11 | async-start | bytes 1638400 | tf_op jit(solution)/shard_map/reduce_scatter | solution.py:125
  501.8 8.6 %collective-permute-start.8 = (bf16[128,1280]{1,0:T(8,128)(2,1)}, bf16[128,1280]{1,0:T(8,128)(2,1)S(1)}, u32[]{:S(2)}, u32[]{:S(2)}) collective-permute-start(bf16[128,1280]{1,0:T(8,128)(2,1)} %reduce-scatter.11.cloned.1.call-done), channel_id=1, source_target_pairs={{0,0},{8,32},{16,64},{24,96},{32,8},{40,40},{48,72},{56,104},{64,1... | collective-permute-start | bytes 983048 | tf_op jit(solution)/shard_map/ppermute | solution.py:127
Sparse Core Ops, SparseCore 0:
  27.1 55.8 all-gather.4
  85.9 47.2 all-gather.6
  195.4 32.9 reduce-scatter.8
  245.9 39.5 reduce-scatter.6
  289.1 73.2 reduce-scatter.4
  364.5 30.0 all-gather.8
  397.2 77.0 all-gather.10
  481.5 20.2 reduce-scatter.10

commit v2 on v1

v2 whole, which is shorter than its diff:
```python
import jax
import jax.numpy as jnp
from jax import lax
from jax.experimental import pallas as pl
from jax.experimental.pallas import tpu as pltpu
from jax.sharding import Mesh
from jax.sharding import PartitionSpec as P

HEAD_DIM = 128


BF = jnp.bfloat16
F32 = jnp.float32
MESH = pl.DeviceIdType.MESH
NT = (((1,), (1,)), ((), ()))
TN = (((0,), (0,)), ((), ()))
TY, NY, NM = 4, 4, 8
HEADS, TOK, COLS = 5, 128, 640
QUERIES, KEYS = NM * TOK, NY * TOK
CHUNK = 256
QC = QUERIES // CHUNK
ROWS_W = 160
OUT = NM * ROWS_W
PATCH = 3072
FACTOR = HEAD_DIM ** (-0.5)
LOG2E = 1.4426950408889634


def padded(cells, sides, width):
    for axis, dim in sides:
        count = lax.axis_size(axis)
        ends = count - 1
        head = lax.slice_in_dim(cells, 0, width, axis=dim)
        tail = lax.slice_in_dim(cells, cells.shape[dim] - width, cells.shape[dim], axis=dim)
        cells = jnp.concatenate(
            [
                lax.ppermute(tail, axis, [(i, (i + 1) % count) for i in range(ends)]),
                cells,
                lax.ppermute(head, axis, [((i + 1) % count, i) for i in range(ends)]),
            ],
            axis=dim,
        )
    return cells


def conv(cells, weight, stride):
    return lax.conv_general_dilated(
        cells,
        lax.rev(weight, (0, 1)),
        (stride, stride),
        "VALID",
        dimension_numbers=("NHWC", "HWOI", "NHWC"),
        preferred_element_type=jnp.float32,
    )


def causal(cells, weight, stride):
    own = conv(cells, weight[2], stride)
    later = conv(cells[1:], weight[1], stride)
    return own + jnp.pad(later, ((0, 1), (0, 0), (0, 0), (0, 0)))


def scale_back(pooled, preact, norm_gain):
    scaled = norm_gain * preact.astype(jnp.float32)
    sigmoid_val = jax.nn.sigmoid(scaled)
    return (pooled * norm_gain * sigmoid_val * (1.0 + scaled * (1.0 - sigmoid_val))).astype(
        jnp.bfloat16
    )


def mm(one, two, dims=(((1,), (0,)), ((), ()))):
    return lax.dot_general(one, two, dims, preferred_element_type=F32)


def attend_kernel(
    patches, patch_w, query, key, value, weight, out,
    p_all, pw, q_all, k_all, v_all, g_all, w_all, probs, gp, stat_s, stat_r, dot_s, dot_r,
    dq_s, dq_r, dk_s, dk_r, dv_s, dv_r, a_all, part, red,
    sem_p, sem_q, sem_k, sem_v, sem_w, sem_g, sem_st, sem_rd, sem_dq, sem_dk, sem_dv, sem_a, sem_o, sem_l,
):
    c, y, m = lax.axis_index("ty"), lax.axis_index("y"), lax.axis_index("m")

    def in_c(step):
        return (lax.rem(c + step, TY), y, m)

    def in_y(step):
        return (c, lax.rem(y + step, NY), m)

    def in_m(step):
        return (c, y, lax.rem(m + step, NM))

    def rows(index, size=TOK):
        return pl.ds(pl.multiple_of(index * size, size), size)

    def cols(h):
        return pl.ds(pl.multiple_of(h * HEAD_DIM, HEAD_DIM), HEAD_DIM)

    def push(src, dst, sems, index, target):
        return pltpu.make_async_remote_copy(
            src_ref=src, dst_ref=dst, send_sem=sems.at[0, index], recv_sem=sems.at[1, index],
            device_id=target, device_id_type=MESH,
        )

    barrier = pltpu.get_barrier_semaphore()
    for dc in range(TY):
        for dy in range(NY):
            if dc or dy:
                pl.semaphore_signal(
                    barrier, inc=1, device_id_type=MESH,
                    device_id=(lax.rem(c + dc, TY), lax.rem(y + dy, NY), m),
                )
    for dm in range(1, NM):
        pl.semaphore_signal(barrier, inc=1, device_id=in_m(dm), device_id_type=MESH)

    local = [
        pltpu.make_async_copy(patches, p_all.at[rows(c, 32)], sem_l.at[0]),
        pltpu.make_async_copy(query, q_all.at[rows(m)], sem_l.at[1]),
        pltpu.make_async_copy(key, k_all.at[rows(y)], sem_l.at[2]),
        pltpu.make_async_copy(value, v_all.at[rows(y)], sem_l.at[3]),
        pltpu.make_async_copy(weight, w_all.at[:, rows(m, ROWS_W)], sem_l.at[4]),
        pltpu.make_async_copy(patch_w, pw, sem_l.at[5]),
    ]
    for copy in local:
        copy.start()
    pl.semaphore_wait(barrier, TY * NY - 1 + NM - 1)

    to_p = [push(patches, p_all.at[rows(c, 32)], sem_p, d, in_c(d)) for d in range(1, TY)]
    to_k = [push(key, k_all.at[rows(y)], sem_k, d, in_y(d)) for d in range(1, NY)]
    to_q = [push(query, q_all.at[rows(m)], sem_q, d, in_m(d)) for d in range(1, NM)]
    to_v = [push(value, v_all.at[rows(y)], sem_v, d, in_y(d)) for d in range(1, NY)]
    to_w = [push(weight, w_all.at[:, rows(m, ROWS_W)], sem_w, d, in_m(d)) for d in range(1, NM)]
    for copy in to_p + to_k + to_q + to_v + to_w:
        copy.start()

    for copy in local:
        copy.wait()
    for copy in to_p:
        copy.wait_recv()
    g_all[rows(m), :] = mm(p_all[...], pw[...]).astype(BF)
    to_g = [push(g_all.at[rows(m)], g_all.at[rows(m)], sem_g, d, in_m(d)) for d in range(1, NM)]
    for copy in to_g:
        copy.start()

    for copy in to_k + to_q:
        copy.wait_recv()

    def score_step(i, _):
        h, qc = i // QC, lax.rem(i, QC)
        span = rows(qc, CHUNK)
        s = mm(k_all[:, cols(h)], q_all[span, cols(h)], NT) * (FACTOR * LOG2E)
        peak = jnp.max(s, axis=0, keepdims=True)
        e = jnp.exp2(s - peak)
        stat_s[h, :, span] = peak
        stat_s[HEADS + h, :, span] = jnp.sum(e, axis=0, keepdims=True)
        probs[h, :, span] = e.astype(BF)
        return 0

    lax.fori_loop(0, HEADS * QC, score_step, 0)
    to_st = [push(stat_s, stat_r.at[m], sem_st, d, in_m(d)) for d in range(1, NM)]
    for copy in to_st:
        copy.start()
    stat_r[m] = stat_s[...]
    for copy in to_st + to_v + to_g:
        copy.wait_recv()

    def grad_step(i, _):
        h, qc = i // QC, lax.rem(i, QC)
        span = rows(qc, CHUNK)
        peaks = [stat_r[j, h, :, span] for j in range(NM)]
        top = peaks[0]
        for j in range(1, NM):
            top = jnp.maximum(top, peaks[j])
        total = jnp.zeros_like(top)
        for j in range(NM):
            total = total + stat_r[j, HEADS + h, :, span] * jnp.exp2(peaks[j] - top)
        share = jnp.exp2(stat_s[h, :, span] - top) / total
        p = probs[h, :, span].astype(F32) * share
        g = mm(v_all[:, cols(h)], g_all[span, cols(h)], NT)
        dot_s[h, :, span] = jnp.sum(p * g, axis=0, keepdims=True)
        probs[h, :, span] = p.astype(BF)
        gp[h, :, span] = g.astype(BF)
        return 0

    lax.fori_loop(0, HEADS * QC, grad_step, 0)
    to_rd = [push(dot_s, dot_r.at[m], sem_rd, d, in_m(d)) for d in range(1, NM)]
    for copy in to_rd:
        copy.start()
    dot_r[m] = dot_s[...]

    def dv_copies(h):
        return [
            push(dv_s.at[rows(lax.rem(y + d, NY)), cols(h)], dv_r.at[rows(y), cols(h)], sem_dv, h * NY + d, in_y(d))
            for d in range(1, NY)
        ]

    def dk_copies(h):
        return [
            push(dk_s.at[rows(lax.rem(y + d, NY)), cols(h)], dk_r.at[rows(y), cols(h)], sem_dk, h * NY + d, in_y(d))
            for d in range(1, NY)
        ]

    def dq_copies(h):
        return [
            push(dq_s.at[rows(lax.rem(m + d, NM)), cols(h)], dq_r.at[rows(m), cols(h)], sem_dq, h * NM + d, in_m(d))
            for d in range(1, NM)
        ]

    def a_copies(h):
        return [
            push(a_all.at[:, rows(y), cols(h)], a_all.at[:, rows(y), cols(h)], sem_a, h * NY + d, in_y(d))
            for d in range(1, NY)
        ]

    def value_step(h, _):
        dv_s[:, cols(h)] = mm(probs[h], g_all[:, cols(h)]).astype(BF)
        for copy in dv_copies(h):
            copy.start()
        return 0

    lax.fori_loop(0, HEADS, value_step, 0)
    for copy in to_rd:
        copy.wait_recv()

    def key_step(h, _):
        for qc in range(QC):
            span = pl.ds(qc * CHUNK, CHUNK)
            dot = dot_r[0, h, :, span]
            for j in range(1, NM):
                dot = dot + dot_r[j, h, :, span]
            ds = (probs[h, :, span].astype(F32) * (gp[h, :, span].astype(F32) - dot)).astype(BF)
            gp[h, :, span] = ds
            dq_s[span, cols(h)] = (FACTOR * mm(ds, k_all[:, cols(h)], TN)).astype(BF)
        for copy in dq_copies(h):
            copy.start()
        dk_s[:, cols(h)] = (FACTOR * mm(gp[h], q_all[:, cols(h)])).astype(BF)
        for copy in dk_copies(h):
            copy.start()
        return 0

    lax.fori_loop(0, HEADS, key_step, 0)

    def sum_step(h, _):
        for copy in dq_copies(h) + dk_copies(h) + dv_copies(h):
            copy.wait_recv()
        dq = dq_s[rows(m), cols(h)].astype(F32)
        for d in range(1, NM):
            dq = dq + dq_r[rows(lax.rem(m + d, NM)), cols(h)].astype(F32)
        dk = dk_s[rows(y), cols(h)].astype(F32)
        dv = dv_s[rows(y), cols(h)].astype(F32)
        for d in range(1, NY):
            other = rows(lax.rem(y + d, NY))
            dk = dk + dk_r[other, cols(h)].astype(F32)
            dv = dv + dv_r[other, cols(h)].astype(F32)
        a_all[0, rows(y), cols(h)] = dq.astype(BF)
        a_all[1, rows(y), cols(h)] = dk.astype(BF)
        a_all[2, rows(y), cols(h)] = dv.astype(BF)
        for copy in a_copies(h):
            copy.start()
        return 0

    lax.fori_loop(0, HEADS, sum_step, 0)
    for copy in to_w:
        copy.wait_recv()

    def arrive(h, _):
        for copy in a_copies(h):
            copy.wait_recv()
        return 0

    lax.fori_loop(0, HEADS, arrive, 0)

    def out_copy(n, d):
        span = pl.ds(pl.multiple_of(n * CHUNK, CHUNK), CHUNK)
        to = lax.rem(y + d, NY)
        return pltpu.make_async_remote_copy(
            src_ref=part.at[rows(to), span], dst_ref=red.at[rows(c), span],
            send_sem=sem_o.at[0, n * NY + d], recv_sem=sem_o.at[1, n * NY + c],
            device_id=(y, to, m), device_id_type=MESH,
        )

    def project(n, _):
        span = pl.ds(pl.multiple_of(n * CHUNK, CHUNK), CHUNK)
        total = mm(a_all[0], w_all[0, span, :], NT)
        total = total + mm(a_all[1], w_all[1, span, :], NT)
        total = total + mm(a_all[2], w_all[2, span, :], NT)
        part[:, span] = total.astype(BF)
        for d in range(1, NY):
            out_copy(n, d).start()

        @pl.when(c == y)
        def _():
            red[rows(c), span] = part[rows(y), span]

        @pl.when(c != y)
        def _():
            out_copy(n, 0).start()

        return 0

    lax.fori_loop(0, OUT // CHUNK, project, 0)

    step = lax.rem(y - c + NY, NY)

    def finish(n, _):
        span = pl.ds(pl.multiple_of(n * CHUNK, CHUNK), CHUNK)
        for other in range(TY):
            @pl.when((c != y) | (c != other))
            def _():
                pltpu.make_async_remote_copy(
                    src_ref=part.at[rows(0), span], dst_ref=red.at[rows(other), span],
                    send_sem=sem_o.at[0, n * NY], recv_sem=sem_o.at[1, n * NY + other],
                    device_id=in_y(1), device_id_type=MESH,
                ).wait_recv()
        total = red[rows(0), span].astype(F32)
        for other in range(1, TY):
            total = total + red[rows(other), span].astype(F32)
        out[:, span] = total.astype(BF)
        return 0

    lax.fori_loop(0, OUT // CHUNK, finish, 0)

    for copy in to_p + to_k + to_q + to_v + to_w + to_g + to_st + to_rd:
        copy.wait_send()

    def sent(h, _):
        for copy in dv_copies(h) + dk_copies(h) + dq_copies(h) + a_copies(h):
            copy.wait_send()
        return 0

    lax.fori_loop(0, HEADS, sent, 0)

    def out_sent(n, _):
        for d in range(1, NY):
            out_copy(n, d).wait_send()

        @pl.when(c != y)
        def _():
            out_copy(n, 0).wait_send()

        return 0

    lax.fori_loop(0, OUT // CHUNK, out_sent, 0)


def body(
    out_grad,
    preact,
    norm_gain,
    mid_weight,
    up_weight,
    patch_weight,
    query_proj,
    key_proj,
    value_proj,
    qkv_weight,
):
    fine = padded(out_grad, (("ty", 1), (("y", "m"), 2)), 1).astype(F32)
    fine = fine[:, :-1] + fine[:, 1:]
    fine = (fine[:, :, :-1] + fine[:, :, 1:]).astype(BF)
    pooled = causal(fine, up_weight, 2)
    mid_grad = scale_back(pooled, preact, norm_gain)
    mid_pad = padded(mid_grad, (("ty", 1), (("y", "m"), 2)), 1)
    feature_grad = causal(mid_pad, mid_weight, 1).astype(BF)
    frame_count, tile_rows, tile_cols, channels = feature_grad.shape
    patches = feature_grad.reshape(frame_count, tile_rows // 2, 2, tile_cols // 2, 2, channels)
    patches = patches.transpose(1, 3, 0, 2, 4, 5).reshape(
        tile_rows // 2 * (tile_cols // 2), frame_count * 4 * channels
    )
    any_space = pl.BlockSpec(memory_space=pl.ANY)

    def sems(count):
        return pltpu.SemaphoreType.DMA((2, count))

    latent_grad = pl.pallas_call(
        attend_kernel,
        out_shape=jax.ShapeDtypeStruct((TOK, OUT), BF),
        in_specs=[any_space] * 6,
        out_specs=pl.BlockSpec(memory_space=pltpu.VMEM),
        scratch_shapes=[
            pltpu.VMEM((TOK, PATCH), BF),
            pltpu.VMEM((PATCH, COLS), BF),
            pltpu.VMEM((QUERIES, COLS), BF),
            pltpu.VMEM((KEYS, COLS), BF),
            pltpu.VMEM((KEYS, COLS), BF),
            pltpu.VMEM((QUERIES, COLS), BF),
            pltpu.VMEM((3, OUT, COLS), BF),
            pltpu.VMEM((HEADS, KEYS, QUERIES), BF),
            pltpu.VMEM((HEADS, KEYS, QUERIES), BF),
            pltpu.VMEM((2 * HEADS, 1, QUERIES), F32),
            pltpu.VMEM((NM, 2 * HEADS, 1, QUERIES), F32),
            pltpu.VMEM((HEADS, 1, QUERIES), F32),
            pltpu.VMEM((NM, HEADS, 1, QUERIES), F32),
            pltpu.VMEM((QUERIES, COLS), BF),
            pltpu.VMEM((QUERIES, COLS), BF),
            pltpu.VMEM((KEYS, COLS), BF),
            pltpu.VMEM((KEYS, COLS), BF),
            pltpu.VMEM((KEYS, COLS), BF),
            pltpu.VMEM((KEYS, COLS), BF),
            pltpu.VMEM((3, KEYS, COLS), BF),
            pltpu.VMEM((KEYS, OUT), BF),
            pltpu.VMEM((KEYS, OUT), BF),
            sems(TY),
            sems(NM),
            sems(NY),
            sems(NY),
            sems(NM),
            sems(NM),
            sems(NM),
            sems(NM),
            sems(HEADS * NM),
            sems(HEADS * NY),
            sems(HEADS * NY),
            sems(HEADS * NY),
            sems(OUT // CHUNK * NY),
            pltpu.SemaphoreType.DMA((6,)),
        ],
        compiler_params=pltpu.CompilerParams(
            collective_id=0, has_side_effects=True, vmem_limit_bytes=56 * 1024 * 1024
        ),
        name="attend",
    )(patches, patch_weight, query_proj, key_proj, value_proj, qkv_weight.transpose(1, 0, 2))
    return (feature_grad, latent_grad)


def solution(mesh):
    rows, cols = mesh.devices.shape
    split = Mesh(mesh.devices.reshape(rows, rows, cols // rows), ("ty", "y", "m"))
    tx = ("y", "m")
    placed = (
        P(None, "ty", tx, None),
        P(None, "ty", tx, None),
        P(),
        P(),
        P(),
        P(None, "ty"),
        P(tx, "ty"),
        P(tx, "ty"),
        P(tx, "ty"),
        P(tx, None, "ty"),
    )
    return jax.shard_map(
        body,
        mesh=split,
        in_specs=placed,
        out_specs=(P(None, "ty", tx, None), P(tx, "ty")),
        check_vma=False,
    )
```

time: 523 us -> 255 us (0.49)
  waiting for transfers between devices: 250 us -> 12.7 us
  Pallas kernels: 0 us -> 195 us
  blocking collectives: 141 us -> 0 us
  matrix products: 49.5 us -> 9.02 us
  other arithmetic: 17.7 us -> 2.18 us
  between operations: 14.6 us -> 0.94 us
  starting transfers between devices: 31.2 us -> 24.4 us
  local copies, waits for them, and re-layouts: 13.6 us -> 7.52 us
    pallas_call x0 -> x1, Pallas kernels: none -> 195 us  [body(): pl.pallas_call(attend_kernel, out_shape=jax.ShapeDtypeStruct((TOK, OUT),...]
    reduce_scatter x4 -> x0, waiting for transfers between devices: 132 us -> none  [the longest x3 111 us: scatter(): return lax.psum_scatter(rows, axis, scatter_dimension=0, tiled=True)]
    all_gather x4 -> x0, waiting for transfers between devices: 109 us -> none  [the longest x1 79.7 us: body(): w_all = lax.all_gather(qkv_weight, 'm', axis=0, tiled=True)]
    psum x2 -> x0, blocking collectives: 60.4 us -> none  [the longest x1 30.5 us: body(): row_dot = lax.psum(jnp.sum(probs * grad_probs, axis=-1, keepdims=True), 'm')]
    all_gather x3 -> x0, blocking collectives: 50.2 us -> none  [the longest x1 22 us: body(): key_all = lax.all_gather(key_proj, 'y', axis=0, tiled=True)]
    dot_general x7 -> x0, matrix products: 37.1 us -> none  [the longest x5 26.5 us: dots(): return jnp.einsum(spec, one, two, preferred_element_type=f32)]
    pmax x1 -> x0, blocking collectives: 30.5 us -> none  [body(): peak = lax.pmax(jnp.max(scores, axis=-1, keepdims=True), 'm')]
    ppermute x4, waiting for transfers between devices: 2.03 us -> 12.7 us  [padded(): lax.ppermute(head, axis, [((i + 1) % count, i) for i in range(ends)])]
  transfers between devices with their start and end apart: 17 -> 8, of which waited for: 9 -> 4; matrix products, arithmetic and copies ran while one was open for 12% -> 1% of each run, Pallas kernels for 0% -> 0%
where the time goes in v2:
time: 255 us; the launch traced here: 252 us
  Pallas kernels  195 us (76%)
  starting transfers between devices  24.4 us (10%)
  waiting for transfers between devices  12.7 us (5%)
  matrix products  9.02 us (4%)
  local copies, waits for them, and re-layouts  7.52 us (3%)
    pallas_call x1, Pallas kernels, body(): pl.pallas_call(attend_kernel, out_shape=jax.ShapeDtypeStruct((TOK, OUT),...  195 us
    ppermute x4, starting transfers between devices, padded(): lax.ppermute(tail, axis, [(i, (i + 1) % count) for i in range(ends)])  17.8 us
    ppermute x4, waiting for transfers between devices, padded(): lax.ppermute(head, axis, [((i + 1) % count, i) for i in range(ends)])  12.7 us
    conv_general_dilated x4, matrix products, conv(): lax.conv_general_dilated(cells, lax.rev(weight, (0, 1)), (stride, stride)...  9.02 us
    ppermute x4, starting transfers between devices, padded(): lax.ppermute(head, axis, [((i + 1) % count, i) for i in range(ends)])  6.61 us
  transfers between devices with their start and end apart: 8, of which 4 were waited for; matrix products, arithmetic and copies ran while one was open for 1% of the time, Pallas kernels for 0%

profile of v2, /device:TPU:1, one launch (start us, length us, event | category | flops | bytes accessed | tf_op | source)
XLA Modules:
  0.0 251.8 jit_solution(15543507164098675750)
XLA Ops:
  0.6 0.7 fusion.25
  1.4 4.9 %collective-permute-start = (bf16[2,1,16,192]{3,0,2,1:T(2,128)(2,1)S(1)}, bf16[2,1,16,192]{3,0,2,1:T(2,128)(2,1)S(1)}, u32[]{:S(2)}, u32[]{:S(2)}) collective-permute-start(bf16[2,1,16,192]{3,0,2,1:T(2,128)(2,1)S(1)} %copy.42), channel_id=1, source_target_pairs={{0,32},{32,64},{64,96},{1,33},{33,65},{65,97},{2,34},{34,66},{66,9... | collective-permute-start | bytes 36872 | tf_op jit(solution)/shard_map/ppermute | solution.py:37
  6.4 1.9 collective-permute-start.1
  8.3 0.0 collective-permute-done
  8.3 1.6 constant_dynamic-update-slice_fusion.1
  9.9 1.5 collective-permute-done.1
  11.4 0.1 fusion.24
  11.5 5.2 %collective-permute-start.2 = (bf16[2,34,1,192]{3,0,2,1:T(2,128)(2,1)S(1)}, bf16[2,34,1,192]{3,0,2,1:T(2,128)(2,1)S(1)}, u32[]{:S(2)}, u32[]{:S(2)}) collective-permute-start(bf16[2,34,1,192]{3,0,2,1:T(2,128)(2,1)S(1)} %get-tuple-element.6), channel_id=1, source_target_pairs={{0,1},{1,2},{2,3},{3,4},{4,5},{5,6},{6,7},{7,8},{8,9},{9,10},{10,1... | collective-permute-start | bytes 78344 | tf_op jit(solution)/shard_map/ppermute | solution.py:37
  16.7 1.3 collective-permute-start.3
  18.0 1.5 slice_bitcast_fusion
  19.5 0.1 rev.8
  19.6 0.0 collective-permute-done.2
  19.6 3.3 %collective-permute-done.3 = bf16[2,34,1,192]{3,0,2,1:T(2,128)(2,1)S(1)} collective-permute-done((bf16[2,34,1,192]{3,0,2,1:T(2,128)(2,1)S(1)}, bf16[2,34,1,192]{3,0,2,1:T(2,128)(2,1)S(1)}, u32[]{:S(2)}, u32[]{:S(2)}) %collective-permute-start.3) | collective-permute-done | bytes 26144 | tf_op jit(solution)/shard_map/ppermute | solution.py:39
  22.9 0.8 maximum_convert_fusion
  23.7 0.4 slice_add_fusion
  24.2 0.4 fusion.9
  24.6 0.0 slice-start
  24.6 3.1 %fusion.6 = f32[2,16,8,384]{3,0,2,1:T(2,128)S(1)} fusion(bf16[2,33,17,192]{3,0,2,1:T(2,128)(2,1)S(1)} %fusion.9, bf16[3,3,3,384,192]{3,4,2,1,0:T(8,128)(2,1)} %param.14), kind=kOutput, calls=%fused_computation.6 | convolution fusion | flops 339738624 | bytes 2151168 | tf_op jit(solution)/shard_map/conv_general_dilated | solution.py:47
  27.7 0.0 copy-start
  27.7 0.0 copy-start.1
  27.7 0.0 slice-start.1
  27.7 1.6 fusion.16
  29.4 0.0 copy-done
  29.4 0.0 copy-done.1
  29.4 0.2 fusion.21
  29.6 3.0 %collective-permute-start.4 = (bf16[2,1,8,384]{3,2,1,0:T(8,128)(2,1)S(1)}, bf16[2,1,8,384]{3,2,1,0:T(8,128)(2,1)S(1)}, u32[]{:S(2)}, u32[]{:S(2)}) collective-permute-start(bf16[2,1,8,384]{3,2,1,0:T(8,128)(2,1)S(1)} %get-tuple-element.12), channel_id=1, source_target_pairs={{0,32},{32,64},{64,96},{1,33},{33,65},{65,97},{2,34},{34,66},{66,9... | collective-permute-start | bytes 36872 | tf_op jit(solution)/shard_map/ppermute | solution.py:37
  32.6 1.9 collective-permute-start.5
  34.5 0.0 collective-permute-done.4
  34.5 3.1 %collective-permute-done.5 = bf16[2,1,8,384]{3,2,1,0:T(8,128)(2,1)S(1)} collective-permute-done((bf16[2,1,8,384]{3,2,1,0:T(8,128)(2,1)S(1)}, bf16[2,1,8,384]{3,2,1,0:T(8,128)(2,1)S(1)}, u32[]{:S(2)}, u32[]{:S(2)}) %collective-permute-start.5) | collective-permute-done | bytes 12320 | tf_op jit(solution)/shard_map/ppermute | solution.py:39
  37.6 0.1 pad_maximum_fusion.3
  37.7 4.6 %collective-permute-start.6 = (bf16[2,18,1,384]{3,2,1,0:T(2,128)(2,1)S(1)}, bf16[2,18,1,384]{3,2,1,0:T(2,128)(2,1)S(1)}, u32[]{:S(2)}, u32[]{:S(2)}) collective-permute-start(bf16[2,18,1,384]{3,2,1,0:T(2,128)(2,1)S(1)} %get-tuple-element.10), channel_id=1, source_target_pairs={{0,1},{1,2},{2,3},{3,4},{4,5},{5,6},{6,7},{7,8},{8,9},{9,10},{10,1... | collective-permute-start | bytes 82952 | tf_op jit(solution)/shard_map/ppermute | solution.py:37
  42.3 1.5 collective-permute-start.7
  43.8 0.0 collective-permute-done.6
  43.8 4.9 %collective-permute-done.7 = bf16[2,18,1,384]{3,2,1,0:T(2,128)(2,1)S(1)} collective-permute-done((bf16[2,18,1,384]{3,2,1,0:T(2,128)(2,1)S(1)}, bf16[2,18,1,384]{3,2,1,0:T(2,128)(2,1)S(1)}, u32[]{:S(2)}, u32[]{:S(2)}) %collective-permute-start.7) | collective-permute-done | bytes 27680 | tf_op jit(solution)/shard_map/ppermute | solution.py:39
  48.7 0.3 pad_maximum_fusion
  49.0 0.0 slice-done
  49.0 0.0 slice-done.1
  49.0 2.1 fusion
  51.2 2.2 fusion.13
  53.4 0.7 copy.26
  54.1 0.2 copy.44
  54.2 0.8 reshape.12.patches
  55.0 195.0 %attend.1 = bf16[128,1280]{1,0:T(8,128)(2,1)} custom-call(bf16[32,3072]{1,0:T(8,128)(2,1)} %reshape.12.patches, bf16[3072,640]{1,0:T(8,128)(2,1)} %patch_w.1, bf16[128,640]{1,0:T(8,128)(2,1)} %query.1, bf16[128,640]{1,0:T(8,128)(2,1)} %key.1, bf16[128,640]{1,0:T(8,128)(2,1)} %value.1, bf16[3,160,640]{2,1,0:T(8,128)(2,1)} %bitcast.24), custom_call_target="tpu_custom_call" | custom-call | tf_op jit(solution)/shard_map/attend/pallas_call | solution.py:374
  250.0 1.7 copy.48
  (8 shorter events, 0.1 us)
Async XLA Ops:
  1.4 6.9 %collective-permute-start = (bf16[2,1,16,192]{3,0,2,1:T(2,128)(2,1)S(1)}, bf16[2,1,16,192]{3,0,2,1:T(2,128)(2,1)S(1)}, u32[]{:S(2)}, u32[]{:S(2)}) collective-permute-start(bf16[2,1,16,192]{3,0,2,1:T(2,128)(2,1)S(1)} %copy.42), channel_id=1, source_target_pairs={{0,32},{32,64},{64,96},{1,33},{33,65},{65,97},{2,34},{34,66},{66,9... | collective-permute-start | bytes 36872 | tf_op jit(solution)/shard_map/ppermute | solution.py:37
  6.4 5.1 %collective-permute-start.1 = (bf16[2,1,16,192]{3,0,2,1:T(2,128)(2,1)S(1)}, bf16[2,1,16,192]{3,0,2,1:T(2,128)(2,1)S(1)}, u32[]{:S(2)}, u32[]{:S(2)}) collective-permute-start(bf16[2,1,16,192]{3,0,2,1:T(2,128)(2,1)S(1)} %copy.43), channel_id=1, source_target_pairs={{32,0},{64,32},{96,64},{33,1},{65,33},{97,65},{34,2},{66,34},{98,6... | collective-permute-start | bytes 36872 | tf_op jit(solution)/shard_map/ppermute | solution.py:39
  11.5 8.1 %collective-permute-start.2 = (bf16[2,34,1,192]{3,0,2,1:T(2,128)(2,1)S(1)}, bf16[2,34,1,192]{3,0,2,1:T(2,128)(2,1)S(1)}, u32[]{:S(2)}, u32[]{:S(2)}) collective-permute-start(bf16[2,34,1,192]{3,0,2,1:T(2,128)(2,1)S(1)} %get-tuple-element.6), channel_id=1, source_target_pairs={{0,1},{1,2},{2,3},{3,4},{4,5},{5,6},{6,7},{7,8},{8,9},{9,10},{10,1... | collective-permute-start | bytes 78344 | tf_op jit(solution)/shard_map/ppermute | solution.py:37
  16.7 6.2 %collective-permute-start.3 = (bf16[2,34,1,192]{3,0,2,1:T(2,128)(2,1)S(1)}, bf16[2,34,1,192]{3,0,2,1:T(2,128)(2,1)S(1)}, u32[]{:S(2)}, u32[]{:S(2)}) collective-permute-start(bf16[2,34,1,192]{3,0,2,1:T(2,128)(2,1)S(1)} %get-tuple-element.7), channel_id=1, source_target_pairs={{1,0},{2,1},{3,2},{4,3},{5,4},{6,5},{7,6},{8,7},{9,8},{10,9},{11,1... | collective-permute-start | bytes 78344 | tf_op jit(solution)/shard_map/ppermute | solution.py:39
  24.6 24.4 %slice-start = ((s8[7962624]{0:T(1024)(128)(4,1)}), s8[4194304]{0:T(1024)(128)(4,1)S(1)}, s32[]{:S(2)}) async-start(s8[7962624]{0:T(1024)(128)(4,1)} %bitcast.25), calls=%async_computation | async-start | bytes 8388608
  27.7 1.7 copy-start
  27.7 1.7 copy-start.1
  27.7 21.3 %slice-start.1 = ((s8[7962624]{0:T(1024)(128)(4,1)}), s8[3768320]{0:T(1024)(128)(4,1)S(1)}, s32[]{:S(2)}) async-start(s8[7962624]{0:T(1024)(128)(4,1)} %bitcast.25), calls=%async_computation.1 | async-start | bytes 7536640
  29.6 4.9 %collective-permute-start.4 = (bf16[2,1,8,384]{3,2,1,0:T(8,128)(2,1)S(1)}, bf16[2,1,8,384]{3,2,1,0:T(8,128)(2,1)S(1)}, u32[]{:S(2)}, u32[]{:S(2)}) collective-permute-start(bf16[2,1,8,384]{3,2,1,0:T(8,128)(2,1)S(1)} %get-tuple-element.12), channel_id=1, source_target_pairs={{0,32},{32,64},{64,96},{1,33},{33,65},{65,97},{2,34},{34,66},{66,9... | collective-permute-start | bytes 36872 | tf_op jit(solution)/shard_map/ppermute | solution.py:37
  32.6 5.0 %collective-permute-start.5 = (bf16[2,1,8,384]{3,2,1,0:T(8,128)(2,1)S(1)}, bf16[2,1,8,384]{3,2,1,0:T(8,128)(2,1)S(1)}, u32[]{:S(2)}, u32[]{:S(2)}) collective-permute-start(bf16[2,1,8,384]{3,2,1,0:T(8,128)(2,1)S(1)} %get-tuple-element.13), channel_id=1, source_target_pairs={{32,0},{64,32},{96,64},{33,1},{65,33},{97,65},{34,2},{66,34},{98,6... | collective-permute-start | bytes 36872 | tf_op jit(solution)/shard_map/ppermute | solution.py:39
  37.7 6.1 %collective-permute-start.6 = (bf16[2,18,1,384]{3,2,1,0:T(2,128)(2,1)S(1)}, bf16[2,18,1,384]{3,2,1,0:T(2,128)(2,1)S(1)}, u32[]{:S(2)}, u32[]{:S(2)}) collective-permute-start(bf16[2,18,1,384]{3,2,1,0:T(2,128)(2,1)S(1)} %get-tuple-element.10), channel_id=1, source_target_pairs={{0,1},{1,2},{2,3},{3,4},{4,5},{5,6},{6,7},{7,8},{8,9},{9,10},{10,1... | collective-permute-start | bytes 82952 | tf_op jit(solution)/shard_map/ppermute | solution.py:37
  42.3 6.4 %collective-permute-start.7 = (bf16[2,18,1,384]{3,2,1,0:T(2,128)(2,1)S(1)}, bf16[2,18,1,384]{3,2,1,0:T(2,128)(2,1)S(1)}, u32[]{:S(2)}, u32[]{:S(2)}) collective-permute-start(bf16[2,18,1,384]{3,2,1,0:T(2,128)(2,1)S(1)} %get-tuple-element.11), channel_id=1, source_target_pairs={{1,0},{2,1},{3,2},{4,3},{5,4},{6,5},{7,6},{8,7},{9,8},{10,9},{11,1... | collective-permute-start | bytes 82952 | tf_op jit(solution)/shard_map/ppermute | solution.py:39

commit v3 on v1

v3 whole, which is shorter than its diff:
```python
import jax
import jax.numpy as jnp
from jax import lax
from jax.experimental import pallas as pl
from jax.experimental.pallas import tpu as pltpu
from jax.sharding import Mesh
from jax.sharding import PartitionSpec as P

HEAD_DIM = 128

BF = jnp.bfloat16
F32 = jnp.float32
MESH = pl.DeviceIdType.MESH
NN = (((1,), (0,)), ((), ()))
NT = (((1,), (1,)), ((), ()))
TN = (((0,), (0,)), ((), ()))
AXES = ("zl", "core", "y", "x", "zh")
SIZES = (2, 2, 4, 4, 2)
NX, NY, NZ, TY = 4, 4, 2, 4
NK = NX * NZ
HEADS, TOK, COLS = 5, 128, 640
FULL = NX * NY * TOK
LAST = NY * TOK
QUERIES = FULL + LAST
KEYS = NK * TOK
CHUNK = 256
FULL_CHUNKS = FULL // CHUNK
CHUNKS = QUERIES // CHUNK
ROWS_W = 160
CUT_W = 64
OUT = NK * ROWS_W
HALF = OUT // 2
PIECES = ((0, 256), (256, 256), (512, 128))
PATCH = 3072
FACTOR = HEAD_DIM ** (-0.5)
LOG2E = 1.4426950408889634


def mm(one, two, dims=NN):
    return lax.dot_general(one, two, dims, preferred_element_type=F32)


def wide(tile):
    return tile.astype(F32)


def attend_kernel(
    patches, patch_w, query, key, value, weight, out,
    p_all, pw, q_all, k_all, v_all, g_own, g_all, w_all, probs, gp, stat_s, stat_r, dot_s, dot_r,
    dq_s, dq_r, dl_r, dk_s, dk_r, dv_s, dv_r, a_all, part, pair, red,
    sem_p, sem_q, sem_k, sem_v, sem_w, sem_g, sem_st, sem_rd, sem_dq, sem_dk, sem_dv, sem_a, sem_c, sem_o, sem_l,
):
    zl, core, y, x, zh = [lax.axis_index(name) for name in AXES]
    c = zl * 2 + core

    def at(dty=0, dy=0, dx=0, dz=0):
        ty = lax.rem(c + dty, TY)
        return (ty // 2, lax.rem(ty, 2), lax.rem(y + dy, NY), lax.rem(x + dx, NX), lax.rem(zh + dz, NZ))

    partner = (zl, 1 - core, y, x, zh)

    def rows(index, size=TOK, base=0):
        return pl.ds(pl.multiple_of(index * size + base, 32), size)

    def cols(h):
        return pl.ds(pl.multiple_of(h * HEAD_DIM, HEAD_DIM), HEAD_DIM)

    def push(src, dst, sems, index, target, arrives=None):
        return pltpu.make_async_remote_copy(
            src_ref=src, dst_ref=dst, send_sem=sems.at[0, index],
            recv_sem=sems.at[1, index if arrives is None else arrives],
            device_id=target, device_id_type=MESH,
        )

    def start(copies):
        for copy in copies:
            copy.start()

    def arrived(copies):
        for copy in copies:
            copy.wait_recv()

    greet = [at(dty=a, dy=b) for a in range(TY) for b in range(NY) if a or b]
    greet += [at(dy=a, dx=b) for a in range(NY) for b in range(1, NX)]
    greet += [at(dx=a, dz=1) for a in range(NX)]
    barrier = pltpu.get_barrier_semaphore()
    for other in greet:
        pl.semaphore_signal(barrier, inc=1, device_id=other, device_id_type=MESH)

    plane = y * NX + x
    line = x * NZ + zh
    local = [
        pltpu.make_async_copy(patches, p_all.at[rows(c, 32)], sem_l.at[0]),
        pltpu.make_async_copy(patch_w, pw, sem_l.at[1]),
        pltpu.make_async_copy(query.at[:, cols(x)], q_all.at[rows(plane)], sem_l.at[2]),
        pltpu.make_async_copy(query.at[:, cols(NX)], q_all.at[rows(y, base=FULL)], sem_l.at[3]),
        pltpu.make_async_copy(key.at[:, cols(x)], k_all.at[rows(line)], sem_l.at[4]),
        pltpu.make_async_copy(key.at[:, cols(NX)], k_all.at[rows(line, base=KEYS)], sem_l.at[5]),
        pltpu.make_async_copy(value.at[:, cols(x)], v_all.at[rows(line)], sem_l.at[6]),
        pltpu.make_async_copy(value.at[:, cols(NX)], v_all.at[rows(line, base=KEYS)], sem_l.at[7]),
        pltpu.make_async_copy(weight, w_all.at[:, rows(line, ROWS_W)], sem_l.at[8]),
    ]
    start(local)
    pl.semaphore_wait(barrier, len(greet))

    def to_queries(src, dst, sems):
        copies = []
        for dy in range(NY):
            for dx in range(NX):
                if dy or dx:
                    head = cols(lax.rem(x + dx, NX))
                    copies.append(push(src.at[:, head], dst.at[rows(plane)], sems, dy * NX + dx, at(dy=dy, dx=dx)))
            if dy:
                copies.append(push(src.at[:, cols(NX)], dst.at[rows(y, base=FULL)], sems, NY * NX + dy, at(dy=dy)))
        return copies

    def to_keys(src, dst, sems):
        copies = []
        for dz in range(NZ):
            for dx in range(NX):
                if dz or dx:
                    head = cols(lax.rem(x + dx, NX))
                    target = at(dx=dx, dz=dz)
                    slot = 2 * (dx * NZ + dz)
                    copies.append(push(src.at[:, head], dst.at[rows(line)], sems, slot, target))
                    copies.append(push(src.at[:, cols(NX)], dst.at[rows(line, base=KEYS)], sems, slot + 1, target))
        return copies

    to_p = [push(patches, p_all.at[rows(c, 32)], sem_p, d, at(dty=d)) for d in range(1, TY)]
    to_k = to_keys(key, k_all, sem_k)
    to_q = to_queries(query, q_all, sem_q)
    to_v = to_keys(value, v_all, sem_v)
    mine = w_all.at[:, rows(line, ROWS_W)]
    to_w = [push(weight, mine, sem_w, d, at(dx=d)) for d in range(1, NX)]
    to_w.append(push(weight, mine, sem_w, 0, at(dz=1)))
    start(to_p + to_k + to_q + to_v + to_w)
    beside = w_all.at[:, pl.ds(pl.multiple_of((x * NZ + 1 - zh) * ROWS_W, 32), CUT_W)]
    on_x = [push(beside, beside, sem_w, NX + d, at(dx=d)) for d in range(1, NX)]
    on_z = []
    for d in range(1, NX):
        first = lax.rem(x - d + NX, NX) * NZ + zh
        below = w_all.at[:, pl.ds(pl.multiple_of(first * ROWS_W + CUT_W, 32), ROWS_W - CUT_W)]
        on_z.append(push(below, below, sem_w, 2 * NX + d, at(dz=1)))

    for copy in local:
        copy.wait()
    arrived(to_p)
    g_own[...] = mm(p_all[...], pw[...]).astype(BF)
    to_g = to_queries(g_own, g_all, sem_g)
    start(to_g)
    g_all[rows(plane), :] = g_own[:, cols(x)]
    g_all[rows(y, base=FULL), :] = g_own[:, cols(NX)]

    arrived(to_k + to_q)

    def spans(i):
        return rows(i, CHUNK), rows(i // FULL_CHUNKS, KEYS)

    def score_step(i, _):
        span, keys = spans(i)
        s = mm(k_all[keys, :], q_all[span, :], NT) * (FACTOR * LOG2E)
        peak = jnp.max(s, axis=0, keepdims=True)
        e = jnp.exp2(s - peak)
        stat_s[0, :, span] = peak
        stat_s[1, :, span] = jnp.sum(e, axis=0, keepdims=True)
        probs[:, span] = e.astype(BF)
        return 0

    lax.fori_loop(0, CHUNKS, score_step, 0)
    to_st = [push(stat_s, stat_r.at[y], sem_st, d, at(dy=d)) for d in range(1, NY)]
    start(to_st)
    stat_r[y] = stat_s[...]
    arrived(to_st)

    def share_step(i, _):
        span, _ = spans(i)
        top = stat_r[0, 0, :, span]
        for j in range(1, NY):
            top = jnp.maximum(top, stat_r[j, 0, :, span])
        total = jnp.zeros_like(top)
        for j in range(NY):
            total = total + stat_r[j, 1, :, span] * jnp.exp2(stat_r[j, 0, :, span] - top)
        share = jnp.exp2(stat_s[0, :, span] - top) / total
        probs[:, span] = (wide(probs[:, span]) * share).astype(BF)
        return 0

    lax.fori_loop(0, CHUNKS, share_step, 0)
    arrived(to_v + to_g)

    def grad_step(i, _):
        span, keys = spans(i)
        g = mm(v_all[keys, :], g_all[span, :], NT)
        dot_s[:, span] = jnp.sum(wide(probs[:, span]) * g, axis=0, keepdims=True)
        gp[:, span] = g.astype(BF)
        return 0

    lax.fori_loop(0, CHUNKS, grad_step, 0)
    to_rd = [push(dot_s, dot_r.at[y], sem_rd, d, at(dy=d)) for d in range(1, NY)]
    start(to_rd)
    dot_r[y] = dot_s[...]

    def key_copies(d, made, got, sems):
        copies = []
        block = lax.rem(x + d, NX) * NZ
        for dz in range(NZ):
            if d or dz:
                there = block + lax.rem(zh + dz, NZ)
                for k in range(2):
                    copies.append(
                        push(made.at[k, rows(there)], got.at[line, k], sems, 2 * (d * NZ + dz) + k, at(dx=d, dz=dz))
                    )
        return copies

    def key_sums(left, right, made, got, sems, scale):
        for d in (2, 1, 3, 0):
            block = rows(lax.rem(x + d, NX), NZ * TOK)
            made[0, block, :] = (scale * mm(left[block, :FULL], right[:FULL, :])).astype(BF)
            made[1, block, :] = (scale * mm(left[block, FULL:], right[FULL:, :])).astype(BF)
            start(key_copies(d, made, got, sems))
        got[line] = made[:, rows(line), :]

    def all_key_copies(made, got, sems):
        return [copy for d in range(NX) for copy in key_copies(d, made, got, sems)]

    key_sums(probs, g_all, dv_s, dv_r, sem_dv, 1.0)
    to_dv = all_key_copies(dv_s, dv_r, sem_dv)
    arrived(to_rd)
    arrived(to_w)
    start(on_x + on_z)

    def query_copies(d):
        copies = []
        there = lax.rem(y + d, NY)
        for dx in range(NX):
            if d or dx:
                block = rows(there * NX + lax.rem(x + dx, NX))
                copies.append(push(dq_s.at[block], dq_r.at[plane], sem_dq, d * NX + dx, at(dy=d, dx=dx)))
        return copies

    def last_copy(d):
        block = rows(lax.rem(y + d, NY), base=FULL)
        return push(dq_s.at[block], dl_r.at[y], sem_dq, NY * NX + d, at(dy=d))

    def query_step(i, _):
        span, keys = spans(i)
        dot = dot_r[0, :, span]
        for j in range(1, NY):
            dot = dot + dot_r[j, :, span]
        ds = (wide(probs[:, span]) * (wide(gp[:, span]) - dot)).astype(BF)
        gp[:, span] = ds
        dq_s[span, :] = (FACTOR * mm(ds, k_all[keys, :], TN)).astype(BF)
        return 0

    for d in (2, 1, 3, 0):
        first = lax.rem(y + d, NY) * 2
        lax.fori_loop(first, first + 2, query_step, 0)
        start(query_copies(d))
    lax.fori_loop(FULL_CHUNKS, CHUNKS, query_step, 0)
    to_dl = [last_copy(d) for d in range(1, NY)]
    start(to_dl)
    dq_r[plane] = dq_s[rows(plane), :]
    dl_r[y] = dq_s[rows(y, base=FULL), :]
    key_sums(gp, q_all, dk_s, dk_r, sem_dk, FACTOR)
    to_dk = all_key_copies(dk_s, dk_r, sem_dk)
    to_dq = [copy for d in range(NY) for copy in query_copies(d)]

    def key_total(part_index, got):
        for h in range(NX):
            total = wide(got[h * NZ, 0])
            for j in range(1, NZ):
                total = total + wide(got[h * NZ + j, 0])
            a_all[part_index, rows(y), h * HEAD_DIM : (h + 1) * HEAD_DIM] = total.astype(BF)
        total = wide(got[0, 1])
        for j in range(1, NK):
            total = total + wide(got[j, 1])
        a_all[part_index, rows(y), NX * HEAD_DIM :] = total.astype(BF)

    def a_copies(k):
        mine = a_all.at[k, rows(y)]
        return [push(mine, mine, sem_a, k * NY + d, at(dy=d)) for d in range(1, NY)]

    to_a = [a_copies(k) for k in range(3)]
    arrived(to_dv)
    key_total(2, dv_r)
    start(to_a[2])
    arrived(to_dq + to_dl)
    for h in range(NX):
        total = wide(dq_r[h])
        for j in range(1, NY):
            total = total + wide(dq_r[j * NX + h])
        a_all[0, rows(y), h * HEAD_DIM : (h + 1) * HEAD_DIM] = total.astype(BF)
    total = wide(dl_r[0])
    for j in range(1, NY):
        total = total + wide(dl_r[j])
    a_all[0, rows(y), NX * HEAD_DIM :] = total.astype(BF)
    start(to_a[0])
    arrived(to_dk)
    key_total(1, dk_r)
    start(to_a[1])
    arrived(on_x + on_z)
    for k in (2, 0, 1):
        arrived(to_a[k])

    def project(first, size):
        span = pl.ds(pl.multiple_of(first, HEAD_DIM), size)
        total = mm(a_all[0], w_all[0, span, :], NT)
        total = total + mm(a_all[1], w_all[1, span, :], NT)
        return total + mm(a_all[2], w_all[2, span, :], NT)

    to_c = []
    for n, (first, size) in enumerate(PIECES):
        part[:, first : first + size] = project((1 - core) * HALF + first, size).astype(BF)
        span = pl.ds(first, size)
        copy = push(part.at[:, span], pair.at[:, span], sem_c, n, partner)
        copy.start()
        to_c.append(copy)

    def out_copy(n, d):
        first, size = PIECES[n]
        to = lax.rem(y + d, NY)
        span = pl.ds(pl.multiple_of(core * HALF + first, HEAD_DIM), size)
        return push(
            pair.at[rows(to), pl.ds(first, size)], red.at[zl, :, span], sem_o, n * NY + d,
            (y // 2, lax.rem(y, 2), to, x, zh), n * NY + c,
        )

    for n, (first, size) in enumerate(PIECES):
        total = project(core * HALF + first, size)
        to_c[n].wait_recv()
        span = pl.ds(first, size)
        pair[:, span] = (total + wide(pair[:, span])).astype(BF)
        for d in (2, 1, 3):
            out_copy(n, d).start()

        @pl.when(c == y)
        def _():
            red[zl, :, pl.ds(pl.multiple_of(core * HALF + first, HEAD_DIM), size)] = pair[rows(y), span]

        @pl.when(c != y)
        def _():
            out_copy(n, 0).start()

    for n, (first, size) in enumerate(PIECES):
        for other in range(TY):
            @pl.when((c != y) | (c != other))
            def _():
                push(
                    pair.at[rows(0), pl.ds(first, size)], red.at[other // 2, :, pl.ds((other % 2) * HALF + first, size)],
                    sem_o, n * NY, at(dy=1), n * NY + other,
                ).wait_recv()
        for half in range(2):
            span = pl.ds(half * HALF + first, size)
            out[:, span] = (wide(red[0, :, span]) + wide(red[1, :, span])).astype(BF)

    done = to_p + to_k + to_q + to_v + to_w + on_x + on_z + to_g + to_st + to_rd + to_dv + to_dq + to_dl + to_dk
    for copy in done + to_a[0] + to_a[1] + to_a[2] + to_c:
        copy.wait_send()
    for n in range(len(PIECES)):
        for d in range(1, NY):
            out_copy(n, d).wait_send()

        @pl.when(c != y)
        def _():
            out_copy(n, 0).wait_send()


def padded(cells, sides, width):
    for axis, dim in sides:
        count = lax.axis_size(axis)
        ends = count - 1
        head = lax.slice_in_dim(cells, 0, width, axis=dim)
        tail = lax.slice_in_dim(cells, cells.shape[dim] - width, cells.shape[dim], axis=dim)
        cells = jnp.concatenate(
            [
                lax.ppermute(tail, axis, [(i, (i + 1) % count) for i in range(ends)]),
                cells,
                lax.ppermute(head, axis, [((i + 1) % count, i) for i in range(ends)]),
            ],
            axis=dim,
        )
    return cells


def conv(cells, weight, stride):
    return lax.conv_general_dilated(
        cells,
        lax.rev(weight, (0, 1)),
        (stride, stride),
        "VALID",
        dimension_numbers=("NHWC", "HWOI", "NHWC"),
        preferred_element_type=jnp.float32,
    )


def causal(cells, weight, stride):
    own = conv(cells, weight[2], stride)
    later = conv(cells[1:], weight[1], stride)
    return own + jnp.pad(later, ((0, 1), (0, 0), (0, 0), (0, 0)))


def scale_back(pooled, preact, norm_gain):
    scaled = norm_gain * preact.astype(jnp.float32)
    sigmoid_val = jax.nn.sigmoid(scaled)
    return (pooled * norm_gain * sigmoid_val * (1.0 + scaled * (1.0 - sigmoid_val))).astype(
        jnp.bfloat16
    )


def body(
    out_grad,
    preact,
    norm_gain,
    mid_weight,
    up_weight,
    patch_weight,
    query_proj,
    key_proj,
    value_proj,
    qkv_weight,
):
    fine = padded(out_grad, ((("zl", "core"), 1), (("y", "x", "zh"), 2)), 1).astype(F32)
    fine = fine[:, :-1] + fine[:, 1:]
    fine = (fine[:, :, :-1] + fine[:, :, 1:]).astype(BF)
    pooled = causal(fine, up_weight, 2)
    mid_grad = scale_back(pooled, preact, norm_gain)
    mid_pad = padded(mid_grad, ((("zl", "core"), 1), (("y", "x", "zh"), 2)), 1)
    feature_grad = causal(mid_pad, mid_weight, 1).astype(BF)
    frame_count, tile_rows, tile_cols, channels = feature_grad.shape
    patches = feature_grad.reshape(frame_count, tile_rows // 2, 2, tile_cols // 2, 2, channels)
    patches = patches.transpose(1, 3, 0, 2, 4, 5).reshape(
        tile_rows // 2 * (tile_cols // 2), frame_count * 4 * channels
    )
    any_space = pl.BlockSpec(memory_space=pl.ANY)

    def sems(count):
        return pltpu.SemaphoreType.DMA((2, count))

    latent_grad = pl.pallas_call(
        attend_kernel,
        out_shape=jax.ShapeDtypeStruct((TOK, OUT), BF),
        in_specs=[any_space] * 6,
        out_specs=pl.BlockSpec(memory_space=pltpu.VMEM),
        scratch_shapes=[
            pltpu.VMEM((TOK, PATCH), BF),
            pltpu.VMEM((PATCH, COLS), BF),
            pltpu.VMEM((QUERIES, HEAD_DIM), BF),
            pltpu.VMEM((2 * KEYS, HEAD_DIM), BF),
            pltpu.VMEM((2 * KEYS, HEAD_DIM), BF),
            pltpu.VMEM((TOK, COLS), BF),
            pltpu.VMEM((QUERIES, HEAD_DIM), BF),
            pltpu.VMEM((3, OUT, COLS), BF),
            pltpu.VMEM((KEYS, QUERIES), BF),
            pltpu.VMEM((KEYS, QUERIES), BF),
            pltpu.VMEM((2, 1, QUERIES), F32),
            pltpu.VMEM((NY, 2, 1, QUERIES), F32),
            pltpu.VMEM((1, QUERIES), F32),
            pltpu.VMEM((NY, 1, QUERIES), F32),
            pltpu.VMEM((QUERIES, HEAD_DIM), BF),
            pltpu.VMEM((NY * NX, TOK, HEAD_DIM), BF),
            pltpu.VMEM((NY, TOK, HEAD_DIM), BF),
            pltpu.VMEM((2, KEYS, HEAD_DIM), BF),
            pltpu.VMEM((NK, 2, TOK, HEAD_DIM), BF),
            pltpu.VMEM((2, KEYS, HEAD_DIM), BF),
            pltpu.VMEM((NK, 2, TOK, HEAD_DIM), BF),
            pltpu.VMEM((3, LAST, COLS), BF),
            pltpu.VMEM((LAST, HALF), BF),
            pltpu.VMEM((LAST, HALF), BF),
            pltpu.VMEM((2, TOK, OUT), BF),
            sems(TY),
            sems(NY * NX + NY),
            sems(2 * NK),
            sems(2 * NK),
            sems(3 * NX),
            sems(NY * NX + NY),
            sems(NY),
            sems(NY),
            sems(NY * NX + NY),
            sems(2 * NK),
            sems(2 * NK),
            sems(3 * NY),
            sems(len(PIECES)),
            sems(len(PIECES) * NY),
            pltpu.SemaphoreType.DMA((9,)),
        ],
        compiler_params=pltpu.CompilerParams(
            collective_id=0, has_side_effects=True, vmem_limit_bytes=56 * 1024 * 1024
        ),
        name="attend",
    )(patches, patch_weight, query_proj, key_proj, value_proj, qkv_weight.transpose(1, 0, 2))
    return (feature_grad, latent_grad)


def solution(mesh):
    split = Mesh(mesh.devices.reshape(SIZES), AXES)
    ty, tx = ("zl", "core"), ("y", "x", "zh")
    placed = (
        P(None, ty, tx, None),
        P(None, ty, tx, None),
        P(),
        P(),
        P(),
        P(None, ty),
        P(tx, ty),
        P(tx, ty),
        P(tx, ty),
        P(tx, None, ty),
    )
    return jax.shard_map(
        body,
        mesh=split,
        in_specs=placed,
        out_specs=(P(None, ty, tx, None), P(tx, ty)),
        check_vma=False,
    )
```

time: 523 us -> 187 us (0.36)
  waiting for transfers between devices: 250 us -> 12.7 us
  blocking collectives: 141 us -> 0 us
  Pallas kernels: 0 us -> 130 us
  matrix products: 49.5 us -> 9.02 us
  other arithmetic: 17.7 us -> 2.18 us
  between operations: 14.6 us -> 0.94 us
  starting transfers between devices: 31.2 us -> 24.4 us
  local copies, waits for them, and re-layouts: 13.6 us -> 7.52 us
    reduce_scatter x4 -> x0, waiting for transfers between devices: 132 us -> none  [the longest x3 111 us: scatter(): return lax.psum_scatter(rows, axis, scatter_dimension=0, tiled=True)]
    pallas_call x0 -> x1, Pallas kernels: none -> 130 us  [body(): pl.pallas_call(attend_kernel, out_shape=jax.ShapeDtypeStruct((TOK, OUT),...]
    all_gather x4 -> x0, waiting for transfers between devices: 109 us -> none  [the longest x1 79.7 us: body(): w_all = lax.all_gather(qkv_weight, 'm', axis=0, tiled=True)]
    psum x2 -> x0, blocking collectives: 60.4 us -> none  [the longest x1 30.5 us: body(): row_dot = lax.psum(jnp.sum(probs * grad_probs, axis=-1, keepdims=True), 'm')]
    all_gather x3 -> x0, blocking collectives: 50.2 us -> none  [the longest x1 22 us: body(): key_all = lax.all_gather(key_proj, 'y', axis=0, tiled=True)]
    dot_general x7 -> x0, matrix products: 37.1 us -> none  [the longest x5 26.5 us: dots(): return jnp.einsum(spec, one, two, preferred_element_type=f32)]
    pmax x1 -> x0, blocking collectives: 30.5 us -> none  [body(): peak = lax.pmax(jnp.max(scores, axis=-1, keepdims=True), 'm')]
    ppermute x4, waiting for transfers between devices: 2.03 us -> 12.7 us  [padded(): lax.ppermute(head, axis, [((i + 1) % count, i) for i in range(ends)])]
  transfers between devices with their start and end apart: 17 -> 8, of which waited for: 9 -> 4; matrix products, arithmetic and copies ran while one was open for 12% -> 2% of each run, Pallas kernels for 0% -> 0%
where the time goes in v3:
time: 187 us
  Pallas kernels  130 us (70%)
  starting transfers between devices  24.4 us (13%)
  waiting for transfers between devices  12.7 us (7%)
  matrix products  9.02 us (5%)
  local copies, waits for them, and re-layouts  7.52 us (4%)
  other arithmetic  2.18 us (1%)
    pallas_call x1, Pallas kernels, body(): pl.pallas_call(attend_kernel, out_shape=jax.ShapeDtypeStruct((TOK, OUT),...  130 us
    ppermute x4, starting transfers between devices, padded(): lax.ppermute(tail, axis, [(i, (i + 1) % count) for i in range(ends)])  17.8 us
    ppermute x4, waiting for transfers between devices, padded(): lax.ppermute(head, axis, [((i + 1) % count, i) for i in range(ends)])  12.7 us
    conv_general_dilated x4, matrix products, conv(): lax.conv_general_dilated(cells, lax.rev(weight, (0, 1)), (stride, stride)...  9.02 us
    ppermute x4, starting transfers between devices, padded(): lax.ppermute(head, axis, [((i + 1) % count, i) for i in range(ends)])  6.61 us
    unnamed x14, local copies, waits for them, and re-layouts  4.11 us
  transfers between devices with their start and end apart: 8, of which 4 were waited for; matrix products, arithmetic and copies ran while one was open for 2% of the time, Pallas kernels for 0%

profile of v3, /device:TPU:1, one launch (start us, length us, event | category | flops | bytes accessed | tf_op | source)
XLA Modules:
  0.0 186.9 jit_solution(6727015296323191911)
XLA Ops:
  0.6 0.7 fusion.25
  1.4 4.9 %collective-permute-start = (bf16[2,1,16,192]{3,0,2,1:T(2,128)(2,1)S(1)}, bf16[2,1,16,192]{3,0,2,1:T(2,128)(2,1)S(1)}, u32[]{:S(2)}, u32[]{:S(2)}) collective-permute-start(bf16[2,1,16,192]{3,0,2,1:T(2,128)(2,1)S(1)} %copy.42), channel_id=1, source_target_pairs={{0,32},{32,64},{64,96},{1,33},{33,65},{65,97},{2,34},{34,66},{66,9... | collective-permute-start | bytes 36872 | tf_op jit(solution)/shard_map/ppermute | solution.py:375
  6.4 1.9 %collective-permute-start.1 = (bf16[2,1,16,192]{3,0,2,1:T(2,128)(2,1)S(1)}, bf16[2,1,16,192]{3,0,2,1:T(2,128)(2,1)S(1)}, u32[]{:S(2)}, u32[]{:S(2)}) collective-permute-start(bf16[2,1,16,192]{3,0,2,1:T(2,128)(2,1)S(1)} %copy.43), channel_id=1, source_target_pairs={{32,0},{64,32},{96,64},{33,1},{65,33},{97,65},{34,2},{66,34},{98,6... | collective-permute-start | bytes 36872 | tf_op jit(solution)/shard_map/ppermute | solution.py:377
  8.3 0.0 collective-permute-done
  8.3 1.6 constant_dynamic-update-slice_fusion.1
  9.9 1.5 collective-permute-done.1
  11.4 0.1 fusion.24
  11.5 5.2 %collective-permute-start.2 = (bf16[2,34,1,192]{3,0,2,1:T(2,128)(2,1)S(1)}, bf16[2,34,1,192]{3,0,2,1:T(2,128)(2,1)S(1)}, u32[]{:S(2)}, u32[]{:S(2)}) collective-permute-start(bf16[2,34,1,192]{3,0,2,1:T(2,128)(2,1)S(1)} %get-tuple-element.6), channel_id=1, source_target_pairs={{0,1},{1,2},{2,3},{3,4},{4,5},{5,6},{6,7},{7,8},{8,9},{9,10},{10,1... | collective-permute-start | bytes 78344 | tf_op jit(solution)/shard_map/ppermute | solution.py:375
  16.7 1.3 collective-permute-start.3
  18.0 1.5 slice_bitcast_fusion
  19.5 0.1 rev.8
  19.6 0.0 collective-permute-done.2
  19.6 3.3 %collective-permute-done.3 = bf16[2,34,1,192]{3,0,2,1:T(2,128)(2,1)S(1)} collective-permute-done((bf16[2,34,1,192]{3,0,2,1:T(2,128)(2,1)S(1)}, bf16[2,34,1,192]{3,0,2,1:T(2,128)(2,1)S(1)}, u32[]{:S(2)}, u32[]{:S(2)}) %collective-permute-start.3) | collective-permute-done | bytes 26144 | tf_op jit(solution)/shard_map/ppermute | solution.py:377
  22.9 0.8 maximum_convert_fusion
  23.7 0.4 slice_add_fusion
  24.2 0.4 fusion.9
  24.6 0.0 slice-start
  24.6 3.1 %fusion.6 = f32[2,16,8,384]{3,0,2,1:T(2,128)S(1)} fusion(bf16[2,33,17,192]{3,0,2,1:T(2,128)(2,1)S(1)} %fusion.9, bf16[3,3,3,384,192]{3,4,2,1,0:T(8,128)(2,1)} %param.14), kind=kOutput, calls=%fused_computation.6 | convolution fusion | flops 339738624 | bytes 2151168 | tf_op jit(solution)/shard_map/conv_general_dilated | solution.py:385
  27.7 0.0 copy-start
  27.7 0.0 copy-start.1
  27.7 0.0 slice-start.1
  27.7 1.6 fusion.16
  29.4 0.0 copy-done
  29.4 0.0 copy-done.1
  29.4 0.2 fusion.21
  29.6 3.0 %collective-permute-start.4 = (bf16[2,1,8,384]{3,2,1,0:T(8,128)(2,1)S(1)}, bf16[2,1,8,384]{3,2,1,0:T(8,128)(2,1)S(1)}, u32[]{:S(2)}, u32[]{:S(2)}) collective-permute-start(bf16[2,1,8,384]{3,2,1,0:T(8,128)(2,1)S(1)} %get-tuple-element.12), channel_id=1, source_target_pairs={{0,32},{32,64},{64,96},{1,33},{33,65},{65,97},{2,34},{34,66},{66,9... | collective-permute-start | bytes 36872 | tf_op jit(solution)/shard_map/ppermute | solution.py:375
  32.6 1.9 %collective-permute-start.5 = (bf16[2,1,8,384]{3,2,1,0:T(8,128)(2,1)S(1)}, bf16[2,1,8,384]{3,2,1,0:T(8,128)(2,1)S(1)}, u32[]{:S(2)}, u32[]{:S(2)}) collective-permute-start(bf16[2,1,8,384]{3,2,1,0:T(8,128)(2,1)S(1)} %get-tuple-element.13), channel_id=1, source_target_pairs={{32,0},{64,32},{96,64},{33,1},{65,33},{97,65},{34,2},{66,34},{98,6... | collective-permute-start | bytes 36872 | tf_op jit(solution)/shard_map/ppermute | solution.py:377
  34.5 0.0 collective-permute-done.4
  34.5 3.1 %collective-permute-done.5 = bf16[2,1,8,384]{3,2,1,0:T(8,128)(2,1)S(1)} collective-permute-done((bf16[2,1,8,384]{3,2,1,0:T(8,128)(2,1)S(1)}, bf16[2,1,8,384]{3,2,1,0:T(8,128)(2,1)S(1)}, u32[]{:S(2)}, u32[]{:S(2)}) %collective-permute-start.5) | collective-permute-done | bytes 12320 | tf_op jit(solution)/shard_map/ppermute | solution.py:377
  37.6 0.1 pad_maximum_fusion.3
  37.7 4.6 %collective-permute-start.6 = (bf16[2,18,1,384]{3,2,1,0:T(2,128)(2,1)S(1)}, bf16[2,18,1,384]{3,2,1,0:T(2,128)(2,1)S(1)}, u32[]{:S(2)}, u32[]{:S(2)}) collective-permute-start(bf16[2,18,1,384]{3,2,1,0:T(2,128)(2,1)S(1)} %get-tuple-element.10), channel_id=1, source_target_pairs={{0,1},{1,2},{2,3},{3,4},{4,5},{5,6},{6,7},{7,8},{8,9},{9,10},{10,1... | collective-permute-start | bytes 82952 | tf_op jit(solution)/shard_map/ppermute | solution.py:375
  42.3 1.5 collective-permute-start.7
  43.8 0.0 collective-permute-done.6
  43.8 4.9 %collective-permute-done.7 = bf16[2,18,1,384]{3,2,1,0:T(2,128)(2,1)S(1)} collective-permute-done((bf16[2,18,1,384]{3,2,1,0:T(2,128)(2,1)S(1)}, bf16[2,18,1,384]{3,2,1,0:T(2,128)(2,1)S(1)}, u32[]{:S(2)}, u32[]{:S(2)}) %collective-permute-start.7) | collective-permute-done | bytes 27680 | tf_op jit(solution)/shard_map/ppermute | solution.py:377
  48.7 0.3 pad_maximum_fusion
  49.0 0.0 slice-done
  49.0 0.0 slice-done.1
  49.0 2.1 %fusion = f32[1,16,8,384]{3,0,2,1:T(1,128)S(1)} fusion(bf16[3,3,3,384,384]{4,3,2,1,0:T(8,128)(2,1)S(1)} %bitcast.26, bf16[1,18,10,384]{3,2,1,0:T(8,128)(2,1)S(1)} %slice.83), kind=kOutput, calls=%fused_computation | convolution fusion | flops 339738624 | bytes 3072000 | tf_op jit(solution)/shard_map/conv_general_dilated | solution.py:385
  51.2 2.2 %fusion.13 = bf16[2,16,8,384]{3,0,2,1:T(2,128)(2,1)S(1)} fusion(bf16[3,3,3,384,384]{4,3,2,1,0:T(8,128)(2,1)S(1)} %bitcast.26, f32[1,16,8,384]{3,0,2,1:T(1,128)S(1)} %fusion, bf16[2,18,10,384]{3,2,1,0:T(8,128)(2,1)S(1)} %pad_maximum_fusion), kind=kOutput, calls=%fused_computation.14 | convolution fusion | flops 679673856 | bytes 3489792 | tf_op jit(solution)/shard_map/conv_general_dilated | solution.py:385
  53.4 0.7 copy.26
  54.1 0.2 copy.44
  54.2 0.8 reshape.12.patches
  55.0 130.1 %attend.1 = bf16[128,1280]{1,0:T(8,128)(2,1)} custom-call(bf16[32,3072]{1,0:T(8,128)(2,1)} %reshape.12.patches, bf16[3072,640]{1,0:T(8,128)(2,1)} %patch_w.1, bf16[128,640]{1,0:T(8,128)(2,1)} %query.1, bf16[128,640]{1,0:T(8,128)(2,1)} %key.1, bf16[128,640]{1,0:T(8,128)(2,1)} %value.1, bf16[3,160,640]{2,1,0:T(8,128)(2,1)} %bitcast.24), custom_call_target="tpu_custom_call" | custom-call | tf_op jit(solution)/shard_map/attend/pallas_call | solution.py:438
  185.2 1.7 copy.48
  (8 shorter events, 0.1 us)
Async XLA Ops:
  1.4 6.9 %collective-permute-start = (bf16[2,1,16,192]{3,0,2,1:T(2,128)(2,1)S(1)}, bf16[2,1,16,192]{3,0,2,1:T(2,128)(2,1)S(1)}, u32[]{:S(2)}, u32[]{:S(2)}) collective-permute-start(bf16[2,1,16,192]{3,0,2,1:T(2,128)(2,1)S(1)} %copy.42), channel_id=1, source_target_pairs={{0,32},{32,64},{64,96},{1,33},{33,65},{65,97},{2,34},{34,66},{66,9... | collective-permute-start | bytes 36872 | tf_op jit(solution)/shard_map/ppermute | solution.py:375
  6.4 5.1 %collective-permute-start.1 = (bf16[2,1,16,192]{3,0,2,1:T(2,128)(2,1)S(1)}, bf16[2,1,16,192]{3,0,2,1:T(2,128)(2,1)S(1)}, u32[]{:S(2)}, u32[]{:S(2)}) collective-permute-start(bf16[2,1,16,192]{3,0,2,1:T(2,128)(2,1)S(1)} %copy.43), channel_id=1, source_target_pairs={{32,0},{64,32},{96,64},{33,1},{65,33},{97,65},{34,2},{66,34},{98,6... | collective-permute-start | bytes 36872 | tf_op jit(solution)/shard_map/ppermute | solution.py:377
  11.5 8.1 %collective-permute-start.2 = (bf16[2,34,1,192]{3,0,2,1:T(2,128)(2,1)S(1)}, bf16[2,34,1,192]{3,0,2,1:T(2,128)(2,1)S(1)}, u32[]{:S(2)}, u32[]{:S(2)}) collective-permute-start(bf16[2,34,1,192]{3,0,2,1:T(2,128)(2,1)S(1)} %get-tuple-element.6), channel_id=1, source_target_pairs={{0,1},{1,2},{2,3},{3,4},{4,5},{5,6},{6,7},{7,8},{8,9},{9,10},{10,1... | collective-permute-start | bytes 78344 | tf_op jit(solution)/shard_map/ppermute | solution.py:375
  16.7 6.2 %collective-permute-start.3 = (bf16[2,34,1,192]{3,0,2,1:T(2,128)(2,1)S(1)}, bf16[2,34,1,192]{3,0,2,1:T(2,128)(2,1)S(1)}, u32[]{:S(2)}, u32[]{:S(2)}) collective-permute-start(bf16[2,34,1,192]{3,0,2,1:T(2,128)(2,1)S(1)} %get-tuple-element.7), channel_id=1, source_target_pairs={{1,0},{2,1},{3,2},{4,3},{5,4},{6,5},{7,6},{8,7},{9,8},{10,9},{11,1... | collective-permute-start | bytes 78344 | tf_op jit(solution)/shard_map/ppermute | solution.py:377
  24.6 24.4 %slice-start = ((s8[7962624]{0:T(1024)(128)(4,1)}), s8[4194304]{0:T(1024)(128)(4,1)S(1)}, s32[]{:S(2)}) async-start(s8[7962624]{0:T(1024)(128)(4,1)} %bitcast.25), calls=%async_computation | async-start | bytes 8388608
  27.7 1.7 copy-start
  27.7 1.7 copy-start.1
  27.7 21.3 %slice-start.1 = ((s8[7962624]{0:T(1024)(128)(4,1)}), s8[3768320]{0:T(1024)(128)(4,1)S(1)}, s32[]{:S(2)}) async-start(s8[7962624]{0:T(1024)(128)(4,1)} %bitcast.25), calls=%async_computation.1 | async-start | bytes 7536640
  29.6 4.9 %collective-permute-start.4 = (bf16[2,1,8,384]{3,2,1,0:T(8,128)(2,1)S(1)}, bf16[2,1,8,384]{3,2,1,0:T(8,128)(2,1)S(1)}, u32[]{:S(2)}, u32[]{:S(2)}) collective-permute-start(bf16[2,1,8,384]{3,2,1,0:T(8,128)(2,1)S(1)} %get-tuple-element.12), channel_id=1, source_target_pairs={{0,32},{32,64},{64,96},{1,33},{33,65},{65,97},{2,34},{34,66},{66,9... | collective-permute-start | bytes 36872 | tf_op jit(solution)/shard_map/ppermute | solution.py:375
  32.6 5.0 %collective-permute-start.5 = (bf16[2,1,8,384]{3,2,1,0:T(8,128)(2,1)S(1)}, bf16[2,1,8,384]{3,2,1,0:T(8,128)(2,1)S(1)}, u32[]{:S(2)}, u32[]{:S(2)}) collective-permute-start(bf16[2,1,8,384]{3,2,1,0:T(8,128)(2,1)S(1)} %get-tuple-element.13), channel_id=1, source_target_pairs={{32,0},{64,32},{96,64},{33,1},{65,33},{97,65},{34,2},{66,34},{98,6... | collective-permute-start | bytes 36872 | tf_op jit(solution)/shard_map/ppermute | solution.py:377
  37.7 6.1 %collective-permute-start.6 = (bf16[2,18,1,384]{3,2,1,0:T(2,128)(2,1)S(1)}, bf16[2,18,1,384]{3,2,1,0:T(2,128)(2,1)S(1)}, u32[]{:S(2)}, u32[]{:S(2)}) collective-permute-start(bf16[2,18,1,384]{3,2,1,0:T(2,128)(2,1)S(1)} %get-tuple-element.10), channel_id=1, source_target_pairs={{0,1},{1,2},{2,3},{3,4},{4,5},{5,6},{6,7},{7,8},{8,9},{9,10},{10,1... | collective-permute-start | bytes 82952 | tf_op jit(solution)/shard_map/ppermute | solution.py:375
  42.3 6.4 %collective-permute-start.7 = (bf16[2,18,1,384]{3,2,1,0:T(2,128)(2,1)S(1)}, bf16[2,18,1,384]{3,2,1,0:T(2,128)(2,1)S(1)}, u32[]{:S(2)}, u32[]{:S(2)}) collective-permute-start(bf16[2,18,1,384]{3,2,1,0:T(2,128)(2,1)S(1)} %get-tuple-element.11), channel_id=1, source_target_pairs={{1,0},{2,1},{3,2},{4,3},{5,4},{6,5},{7,6},{8,7},{9,8},{10,9},{11,1... | collective-permute-start | bytes 82952 | tf_op jit(solution)/shard_map/ppermute | solution.py:377

commit v4 on v3

--- a/solution.py
+++ b/solution.py
@@ -36,6 +36,12 @@
 LOG2E = 1.4426950408889634
 
 
+CH, FINE = 384, 192
+AROUND = ((-1, 0), (1, 0), (0, -1), (0, 1), (-1, -1), (-1, 1), (1, -1), (1, 1))
+ACROSS = (1, 0, 3, 2, 7, 6, 5, 4)
+COLUMNS = NY * NX * NZ
+
+
 def mm(one, two, dims=NN):
     return lax.dot_general(one, two, dims, preferred_element_type=F32)
 
@@ -44,8 +50,10 @@
     return tile.astype(F32)
 
 
-def attend_kernel(
-    patches, patch_w, query, key, value, weight, out,
+def whole_kernel(
+    fine, preact, gain, up_w, mid_w, patch_w, query, key, value, weight, feature, out,
+    g_in, gf, vf, uw, mw, mf, ff, ps, fs_row, fs_col, fs_cor, fr_row, fr_col, fr_cor,
+    ms_row, ms_col, ms_cor, mr_row, mr_col, mr_cor, sem_hf, sem_hm,
     p_all, pw, q_all, k_all, v_all, g_own, g_all, w_all, probs, gp, stat_s, stat_r, dot_s, dot_r,
     dq_s, dq_r, dl_r, dk_s, dk_r, dv_s, dv_r, a_all, part, pair, red,
     sem_p, sem_q, sem_k, sem_v, sem_w, sem_g, sem_st, sem_rd, sem_dq, sem_dk, sem_dv, sem_a, sem_c, sem_o, sem_l,
@@ -83,6 +91,38 @@
     greet = [at(dty=a, dy=b) for a in range(TY) for b in range(NY) if a or b]
     greet += [at(dy=a, dx=b) for a in range(NY) for b in range(1, NX)]
     greet += [at(dx=a, dz=1) for a in range(NX)]
+    place = (y * NX + x) * NZ + zh
+
+    def neighbour(i):
+        ty = lax.rem(c + AROUND[i][0] + TY, TY)
+        t = lax.rem(place + AROUND[i][1] + COLUMNS, COLUMNS)
+        return (ty // 2, lax.rem(ty, 2), t // NK, lax.rem(t // NZ, NX), lax.rem(t, NZ))
+
+    def exists(i):
+        ty, t = c + AROUND[i][0], place + AROUND[i][1]
+        return (ty >= 0) & (ty < TY) & (t >= 0) & (t < COLUMNS)
+
+    def halo_start(made, got, sems):
+        for i in range(8):
+            @pl.when(exists(i))
+            def _():
+                push(made[i], got[ACROSS[i]], sems, i, neighbour(i), ACROSS[i]).start()
+
+            @pl.when(jnp.logical_not(exists(i)))
+            def _():
+                got[i][...] = jnp.zeros(got[i].shape, F32)
+
+    def halo_wait(made, got, sems, sent=False):
+        for i in range(8):
+            @pl.when(exists(i))
+            def _():
+                copy = push(made[i], got[i], sems, i, neighbour(i), i)
+                if sent:
+                    copy.wait_send()
+                else:
+                    copy.wait_recv()
+
+    greet += [neighbour(i) for i in range(2, 8)]
     barrier = pltpu.get_barrier_semaphore()
     for other in greet:
         pl.semaphore_signal(barrier, inc=1, device_id=other, device_id_type=MESH)
@@ -90,7 +130,6 @@
     plane = y * NX + x
     line = x * NZ + zh
     local = [
-        pltpu.make_async_copy(patches, p_all.at[rows(c, 32)], sem_l.at[0]),
         pltpu.make_async_copy(patch_w, pw, sem_l.at[1]),
         pltpu.make_async_copy(query.at[:, cols(x)], q_all.at[rows(plane)], sem_l.at[2]),
         pltpu.make_async_copy(query.at[:, cols(NX)], q_all.at[rows(y, base=FULL)], sem_l.at[3]),
@@ -100,8 +139,31 @@
         pltpu.make_async_copy(value.at[:, cols(NX)], v_all.at[rows(line, base=KEYS)], sem_l.at[7]),
         pltpu.make_async_copy(weight, w_all.at[:, rows(line, ROWS_W)], sem_l.at[8]),
     ]
+    of_conv = [
+        pltpu.make_async_copy(fine, g_in, sem_l.at[0]),
+        pltpu.make_async_copy(up_w.at[pl.ds(1, 2)], uw, sem_l.at[9]),
+        pltpu.make_async_copy(mid_w.at[pl.ds(1, 2)], mw, sem_l.at[10]),
+    ]
+    start(of_conv)
     start(local)
+
+    of_conv[0].wait()
+    lanes = ((0, 0, HEAD_DIM), (1, HEAD_DIM, FINE - HEAD_DIM))
+    for k, first, size in lanes:
+        span = slice(first, first + size)
+        gf[k, :, 0:16, 1, 8:24, :size] = wide(g_in[:, :, 0, :, span])
+        gf[k, :, 1:17, 0, 8:24, :size] = wide(g_in[:, :, 1, :, span])
+        for side, col in ((0, 8), (1, 23)):
+            fs_col[side, :, :, 0, :, span] = gf[k, :, 0:16, 1, col : col + 1, :size]
+            fs_col[side, :, :, 1, :, span] = gf[k, :, 1:17, 0, col : col + 1, :size]
+            fs_cor[side, :, :, span] = gf[k, :, 0, 1, col : col + 1, :size]
+            fs_cor[2 + side, :, :, span] = gf[k, :, 16, 0, col : col + 1, :size]
+    fs_row[0] = wide(g_in[:, 0, 0])
+    fs_row[1] = wide(g_in[:, 15, 1])
     pl.semaphore_wait(barrier, len(greet))
+    f_made = [fs_row.at[0], fs_row.at[1], fs_col.at[0], fs_col.at[1]] + [fs_cor.at[i] for i in range(4)]
+    f_got = [fr_row.at[0], fr_row.at[1], fr_col.at[0], fr_col.at[1]] + [fr_cor.at[i] for i in range(4)]
+    halo_start(f_made, f_got, sem_hf)
 
     def to_queries(src, dst, sems):
         copies = []
@@ -126,14 +188,15 @@
                     copies.append(push(src.at[:, cols(NX)], dst.at[rows(line, base=KEYS)], sems, slot + 1, target))
         return copies
 
-    to_p = [push(patches, p_all.at[rows(c, 32)], sem_p, d, at(dty=d)) for d in range(1, TY)]
+    own_p = p_all.at[rows(c, 32)]
+    to_p = [push(own_p, own_p, sem_p, d, at(dty=d)) for d in range(1, TY)]
     to_k = to_keys(key, k_all, sem_k)
     to_q = to_queries(query, q_all, sem_q)
     to_v = to_keys(value, v_all, sem_v)
     mine = w_all.at[:, rows(line, ROWS_W)]
     to_w = [push(weight, mine, sem_w, d, at(dx=d)) for d in range(1, NX)]
     to_w.append(push(weight, mine, sem_w, 0, at(dz=1)))
-    start(to_p + to_k + to_q + to_v + to_w)
+    start(to_k + to_q + to_v + to_w)
     beside = w_all.at[:, pl.ds(pl.multiple_of((x * NZ + 1 - zh) * ROWS_W, 32), CUT_W)]
     on_x = [push(beside, beside, sem_w, NX + d, at(dx=d)) for d in range(1, NX)]
     on_z = []
@@ -142,8 +205,82 @@
         below = w_all.at[:, pl.ds(pl.multiple_of(first * ROWS_W + CUT_W, 32), ROWS_W - CUT_W)]
         on_z.append(push(below, below, sem_w, 2 * NX + d, at(dz=1)))
 
-    for copy in local:
+    halo_wait(f_made, f_got, sem_hf)
+    for k, first, size in lanes:
+        span = slice(first, first + size)
+        gf[k, :, 0, 0, 8:24, :size] = fr_row[0, :, :, span]
+        gf[k, :, 16, 1, 8:24, :size] = fr_row[1, :, :, span]
+        for side, col in ((0, 7), (1, 24)):
+            gf[k, :, 0:16, 1, col : col + 1, :size] = fr_col[side, :, :, 0, :, span]
+            gf[k, :, 1:17, 0, col : col + 1, :size] = fr_col[side, :, :, 1, :, span]
+            gf[k, :, 0, 0, col : col + 1, :size] = fr_cor[side, :, :, span]
+            gf[k, :, 16, 1, col : col + 1, :size] = fr_cor[2 + side, :, :, span]
+        for f in range(2):
+            four = [gf[k, f, :, :, pl.ds(7 + s, 8, stride=2), :][..., :size] for s in range(4)]
+            for tap in range(3):
+                vf[tap, f, :, :, :, span] = four[2 - tap] + four[3 - tap]
+    of_conv[1].wait()
+
+    def causal(cells, weights, dims):
+        own = later = None
+        for tap in range(9):
+            both = jnp.concatenate([cells(0, tap), cells(1, tap)], axis=0)
+            one = mm(both, weights[1, tap], dims)
+            two = mm(both[TOK:], weights[0, tap], dims)
+            own = one if own is None else own + one
+            later = two if later is None else later + two
+        return own[:TOK] + later, own[TOK:]
+
+    def fine_cells(f, tap):
+        b, col = tap // 3, tap % 3
+        one = vf[col, f, 0:16, 1] if b else vf[col, f, 1:17, 0]
+        two = (vf[col, f, 1:17, 1], vf[col, f, 1:17, 0], vf[col, f, 0:16, 0])[b]
+        return (one + two).reshape(TOK, FINE).astype(BF)
+
+    for f, pooled in enumerate(causal(fine_cells, uw, NN)):
+        z = gain[...] * wide(preact[f].reshape(TOK, CH))
+        s = 1.0 / (1.0 + jnp.exp(-z))
+        mid = (pooled * gain[...] * s * (1.0 + z * (1.0 - s))).astype(BF)
+        mf[f, 1:17, 8:16, :] = wide(mid).reshape(16, 8, CH)
+    ms_row[0] = mf[:, 1, 8:16, :]
+    ms_row[1] = mf[:, 16, 8:16, :]
+    for side, col in ((0, 8), (1, 15)):
+        ms_col[side] = mf[:, 1:17, col : col + 1, :]
+        ms_cor[side] = mf[:, 1, col : col + 1, :]
+        ms_cor[2 + side] = mf[:, 16, col : col + 1, :]
+    m_made = [ms_row.at[0], ms_row.at[1], ms_col.at[0], ms_col.at[1]] + [ms_cor.at[i] for i in range(4)]
+    m_got = [mr_row.at[0], mr_row.at[1], mr_col.at[0], mr_col.at[1]] + [mr_cor.at[i] for i in range(4)]
+    halo_start(m_made, m_got, sem_hm)
+    for copy in local + of_conv[2:]:
         copy.wait()
+    halo_wait(m_made, m_got, sem_hm)
+    mf[:, 0, 8:16, :] = mr_row[0]
+    mf[:, 17, 8:16, :] = mr_row[1]
+    for side, col in ((0, 7), (1, 16)):
+        mf[:, 1:17, col : col + 1, :] = mr_col[side]
+        mf[:, 0, col : col + 1, :] = mr_cor[side]
+        mf[:, 17, col : col + 1, :] = mr_cor[2 + side]
+
+    def mid_cells(f, tap):
+        b, col = tap // 3, tap % 3
+        return mf[f, 2 - b : 18 - b, 9 - col : 17 - col, :].reshape(TOK, CH).astype(BF)
+
+    for f, total in enumerate(causal(mid_cells, mw, NT)):
+        low = total.astype(BF)
+        feature[f] = low.reshape(16, 8, CH)
+        for k in range(3):
+            ff[k, f] = wide(low[:, k * HEAD_DIM : (k + 1) * HEAD_DIM]).reshape(16, 8, HEAD_DIM)
+    for t in range(2):
+        for u in range(2):
+            for w in range(2):
+                first = ((t * 2 + u) * 2 + w) * CH
+                for k in range(3):
+                    span = slice(first + k * HEAD_DIM, first + (k + 1) * HEAD_DIM)
+                    for p in range(8):
+                        ps[p * 4 : p * 4 + 4, span] = ff[k, t, 2 * p + u, pl.ds(w, 4, stride=2), :]
+    p_all[rows(c, 32), :] = ps[...].astype(BF)
+    start(to_p)
+
     arrived(to_p)
     g_own[...] = mm(p_all[...], pw[...]).astype(BF)
     to_g = to_queries(g_own, g_all, sem_g)
@@ -355,6 +492,8 @@
     done = to_p + to_k + to_q + to_v + to_w + on_x + on_z + to_g + to_st + to_rd + to_dv + to_dq + to_dl + to_dk
     for copy in done + to_a[0] + to_a[1] + to_a[2] + to_c:
         copy.wait_send()
+    halo_wait(f_made, f_got, sem_hf, sent=True)
+    halo_wait(m_made, m_got, sem_hm, sent=True)
     for n in range(len(PIECES)):
         for d in range(1, NY):
             out_copy(n, d).wait_send()
@@ -362,48 +501,6 @@
         @pl.when(c != y)
         def _():
             out_copy(n, 0).wait_send()
-
-
-def padded(cells, sides, width):
-    for axis, dim in sides:
-        count = lax.axis_size(axis)
-        ends = count - 1
-        head = lax.slice_in_dim(cells, 0, width, axis=dim)
-        tail = lax.slice_in_dim(cells, cells.shape[dim] - width, cells.shape[dim], axis=dim)
-        cells = jnp.concatenate(
-            [
-                lax.ppermute(tail, axis, [(i, (i + 1) % count) for i in range(ends)]),
-                cells,
-                lax.ppermute(head, axis, [((i + 1) % count, i) for i in range(ends)]),
-            ],
-            axis=dim,
-        )
-    return cells
-
-
-def conv(cells, weight, stride):
-    return lax.conv_general_dilated(
-        cells,
-        lax.rev(weight, (0, 1)),
-        (stride, stride),
-        "VALID",
-        dimension_numbers=("NHWC", "HWOI", "NHWC"),
-        preferred_element_type=jnp.float32,
-    )
-
-
-def causal(cells, weight, stride):
-    own = conv(cells, weight[2], stride)
-    later = conv(cells[1:], weight[1], stride)
-    return own + jnp.pad(later, ((0, 1), (0, 0), (0, 0), (0, 0)))
-
-
-def scale_back(pooled, preact, norm_gain):
-    scaled = norm_gain * preact.astype(jnp.float32)
-    sigmoid_val = jax.nn.sigmoid(scaled)
-    return (pooled * norm_gain * sigmoid_val * (1.0 + scaled * (1.0 - sigmoid_val))).astype(
-        jnp.bfloat16
-    )
 
 
 def body(
@@ -418,29 +515,47 @@
     value_proj,
     qkv_weight,
 ):
-    fine = padded(out_grad, ((("zl", "core"), 1), (("y", "x", "zh"), 2)), 1).astype(F32)
-    fine = fine[:, :-1] + fine[:, 1:]
-    fine = (fine[:, :, :-1] + fine[:, :, 1:]).astype(BF)
-    pooled = causal(fine, up_weight, 2)
-    mid_grad = scale_back(pooled, preact, norm_gain)
-    mid_pad = padded(mid_grad, ((("zl", "core"), 1), (("y", "x", "zh"), 2)), 1)
-    feature_grad = causal(mid_pad, mid_weight, 1).astype(BF)
-    frame_count, tile_rows, tile_cols, channels = feature_grad.shape
-    patches = feature_grad.reshape(frame_count, tile_rows // 2, 2, tile_cols // 2, 2, channels)
-    patches = patches.transpose(1, 3, 0, 2, 4, 5).reshape(
-        tile_rows // 2 * (tile_cols // 2), frame_count * 4 * channels
-    )
     any_space = pl.BlockSpec(memory_space=pl.ANY)
 
     def sems(count):
         return pltpu.SemaphoreType.DMA((2, count))
 
-    latent_grad = pl.pallas_call(
-        attend_kernel,
-        out_shape=jax.ShapeDtypeStruct((TOK, OUT), BF),
-        in_specs=[any_space] * 6,
-        out_specs=pl.BlockSpec(memory_space=pltpu.VMEM),
+    in_vmem = pl.BlockSpec(memory_space=pltpu.VMEM)
+
+    def strips(count, *shape):
+        return pltpu.VMEM((count, 2) + shape, F32)
+
+    return pl.pallas_call(
+        whole_kernel,
+        out_shape=(
+            jax.ShapeDtypeStruct((2, 16, 8, CH), BF),
+            jax.ShapeDtypeStruct((TOK, OUT), BF),
+        ),
+        in_specs=[any_space] + [in_vmem] * 2 + [any_space] * 7,
+        out_specs=(in_vmem, in_vmem),
         scratch_shapes=[
+            pltpu.VMEM((2, 16, 2, 16, FINE), BF),
+            pltpu.VMEM((2, 2, 17, 2, 32, HEAD_DIM), F32),
+            pltpu.VMEM((3, 2, 17, 2, 8, FINE), F32),
+            pltpu.VMEM((2, 9, FINE, CH), BF),
+            pltpu.VMEM((2, 9, CH, CH), BF),
+            pltpu.VMEM((2, 18, 24, CH), F32),
+            pltpu.VMEM((3, 2, 16, 8, HEAD_DIM), F32),
+            pltpu.VMEM((32, PATCH), F32),
+            strips(2, 16, FINE),
+            strips(2, 16, 2, 1, FINE),
+            strips(4, 1, FINE),
+            strips(2, 16, FINE),
+            strips(2, 16, 2, 1, FINE),
+            strips(4, 1, FINE),
+            strips(2, 8, CH),
+            strips(2, 16, 1, CH),
+            strips(4, 1, CH),
+            strips(2, 8, CH),
+            strips(2, 16, 1, CH),
+            strips(4, 1, CH),
+            sems(8),
+            sems(8),
             pltpu.VMEM((TOK, PATCH), BF),
             pltpu.VMEM((PATCH, COLS), BF),
             pltpu.VMEM((QUERIES, HEAD_DIM), BF),
@@ -480,14 +595,24 @@
             sems(3 * NY),
             sems(len(PIECES)),
             sems(len(PIECES) * NY),
-            pltpu.SemaphoreType.DMA((9,)),
+            pltpu.SemaphoreType.DMA((11,)),
         ],
         compiler_params=pltpu.CompilerParams(
             collective_id=0, has_side_effects=True, vmem_limit_bytes=56 * 1024 * 1024
         ),
-        name="attend",
-    )(patches, patch_weight, query_proj, key_proj, value_proj, qkv_weight.transpose(1, 0, 2))
-    return (feature_grad, latent_grad)
+        name="whole",
+    )(
+        out_grad.reshape(2, 16, 2, 16, FINE),
+        preact,
+        norm_gain.reshape(1, CH),
+        up_weight.transpose(0, 1, 2, 4, 3).reshape(3, 9, FINE, CH),
+        mid_weight.reshape(3, 9, CH, CH),
+        patch_weight,
+        query_proj,
+        key_proj,
+        value_proj,
+        qkv_weight.transpose(1, 0, 2),
+    )
 
 
 def solution(mesh):

time: 187 us -> 157 us (0.84)
  starting transfers between devices: 24.4 us -> 0 us
  Pallas kernels: 130 us -> 150 us
  waiting for transfers between devices: 12.7 us -> 0 us
  matrix products: 9.02 us -> 0 us
  local copies, waits for them, and re-layouts: 7.52 us -> 4.59 us
  other arithmetic: 2.18 us -> 0 us
    ppermute x8 -> x0, starting transfers between devices: 24.4 us -> none  [the longest x4 17.8 us: padded(): lax.ppermute(tail, axis, [(i, (i + 1) % count) for i in range(ends)])]
    pallas_call x1, Pallas kernels: 130 us -> 150 us  [body(): pl.pallas_call(whole_kernel, out_shape=(jax.ShapeDtypeStruct((2, 16, 8, C...]
    ppermute x8 -> x0, waiting for transfers between devices: 12.7 us -> none  [the longest x4 12.7 us: padded(): lax.ppermute(head, axis, [((i + 1) % count, i) for i in range(ends)])]
    conv_general_dilated x4 -> x0, matrix products: 9.02 us -> none  [conv(): lax.conv_general_dilated(cells, lax.rev(weight, (0, 1)), (stride, stride)...]
    unnamed x14 -> x2, local copies, waits for them, and re-layouts: 4.11 us -> 3.34 us
  transfers between devices with their start and end apart: 8 -> 0, of which waited for: 4 -> 0; matrix products, arithmetic and copies ran while one was open for 2% -> 0% of each run, Pallas kernels for 0% -> 0%
where the time goes in v4:
time: 157 us; the launch traced here: 155 us
  Pallas kernels  150 us (96%)
  local copies, waits for them, and re-layouts  4.59 us (3%)
    pallas_call x1, Pallas kernels, body(): pl.pallas_call(whole_kernel, out_shape=(jax.ShapeDtypeStruct((2, 16, 8, C...  150 us
    unnamed x2, local copies, waits for them, and re-layouts  3.34 us

profile of v4, /device:TPU:1, one launch (start us, length us, event | category | flops | bytes accessed | tf_op | source)
XLA Modules:
  0.0 155.2 jit_solution(10232454377260240616)
XLA Ops:
  0.6 1.2 reshape.17.gain
  1.9 150.0 %whole.1 = (bf16[2,16,8,384]{3,2,1,0:T(8,128)(2,1)}, bf16[128,1280]{1,0:T(8,128)(2,1)}) custom-call(bf16[2,16,2,16,192]{4,3,2,1,0:T(8,128)(2,1)} %bitcast.9, bf16[2,16,8,384]{3,2,1,0:T(8,128)(2,1)} %preact.1, f32[1,384]{1,0:T(1,128)} %reshape.17.gain, bf16[3,9,192,384]{3,2,1,0:T(8,128)(2,1)} %bitcast.7, bf16[3,9,384,384]{3,2,1,0:T(8,128)(2,1)} %bitcast.6, ...), custom_call_target="tpu_custom_call" | custom-call | tf_op jit(solution)/shard_map/whole/pallas_call | solution.py:528
  151.9 1.6 %copy.14 = bf16[2,16,8,384]{3,2,1,0:T(8,128)(2,1)} copy(bf16[2,16,8,384]{3,2,1,0:T(8,128)(2,1)} %get-tuple-element.4) | data formatting | bytes 393216
  153.5 1.7 %copy.15 = bf16[128,1280]{1,0:T(8,128)(2,1)} copy(bf16[128,1280]{1,0:T(8,128)(2,1)} %get-tuple-element.5) | data formatting | bytes 655360

commit v5 on v4

--- a/solution.py
+++ b/solution.py
@@ -27,7 +27,7 @@
 FULL_CHUNKS = FULL // CHUNK
 CHUNKS = QUERIES // CHUNK
 ROWS_W = 160
-CUT_W = 64
+CUT_W = 48
 OUT = NK * ROWS_W
 HALF = OUT // 2
 PIECES = ((0, 256), (256, 256), (512, 128))
@@ -176,33 +176,45 @@
                 copies.append(push(src.at[:, cols(NX)], dst.at[rows(y, base=FULL)], sems, NY * NX + dy, at(dy=dy)))
         return copies
 
-    def to_keys(src, dst, sems):
+    def keys_over_x(src, dst, sems):
         copies = []
-        for dz in range(NZ):
-            for dx in range(NX):
-                if dz or dx:
-                    head = cols(lax.rem(x + dx, NX))
-                    target = at(dx=dx, dz=dz)
-                    slot = 2 * (dx * NZ + dz)
-                    copies.append(push(src.at[:, head], dst.at[rows(line)], sems, slot, target))
-                    copies.append(push(src.at[:, cols(NX)], dst.at[rows(line, base=KEYS)], sems, slot + 1, target))
+        for d in range(1, NX):
+            head = cols(lax.rem(x + d, NX))
+            copies.append(push(src.at[:, head], dst.at[rows(line)], sems, 2 * d, at(dx=d)))
+            copies.append(push(src.at[:, cols(NX)], dst.at[rows(line, base=KEYS)], sems, 2 * d + 1, at(dx=d)))
         return copies
 
+    def keys_over_z(dst, sems, steps):
+        copies = []
+        for d in steps:
+            block = lax.rem(x - d + NX, NX) * NZ + zh
+            for k in range(2):
+                there = dst.at[rows(block, base=k * KEYS)]
+                copies.append(push(there, there, sems, 2 * NX + 2 * d + k, at(dz=1)))
+        return copies
+
     own_p = p_all.at[rows(c, 32)]
-    to_p = [push(own_p, own_p, sem_p, d, at(dty=d)) for d in range(1, TY)]
-    to_k = to_keys(key, k_all, sem_k)
+    over_z = lax.rem(c + 2, TY)
+    far_p = p_all.at[rows(over_z, 32)]
+    to_p = [push(own_p, own_p, sem_p, 0, at(dty=2)), push(own_p, own_p, sem_p, 1, partner)]
+    on_p = [push(far_p, far_p, sem_p, 2, partner)]
+    kx, vx = keys_over_x(key, k_all, sem_k), keys_over_x(value, v_all, sem_v)
+    kz, vz = keys_over_z(k_all, sem_k, (1, 2, 3)), keys_over_z(v_all, sem_v, (1, 2, 3))
+    own_kz, own_vz = keys_over_z(k_all, sem_k, (0,)), keys_over_z(v_all, sem_v, (0,))
+    to_k, to_v = kx + kz + own_kz, vx + vz + own_vz
     to_q = to_queries(query, q_all, sem_q)
-    to_v = to_keys(value, v_all, sem_v)
     mine = w_all.at[:, rows(line, ROWS_W)]
     to_w = [push(weight, mine, sem_w, d, at(dx=d)) for d in range(1, NX)]
-    to_w.append(push(weight, mine, sem_w, 0, at(dz=1)))
-    start(to_k + to_q + to_v + to_w)
-    beside = w_all.at[:, pl.ds(pl.multiple_of((x * NZ + 1 - zh) * ROWS_W, 32), CUT_W)]
+    to_wz = push(weight, mine, sem_w, 0, at(dz=1))
+    for copy in local:
+        copy.wait()
+    start(kx + own_kz)
+    beside = w_all.at[:, pl.ds(pl.multiple_of((x * NZ + 1 - zh) * ROWS_W, 16), CUT_W)]
     on_x = [push(beside, beside, sem_w, NX + d, at(dx=d)) for d in range(1, NX)]
     on_z = []
     for d in range(1, NX):
         first = lax.rem(x - d + NX, NX) * NZ + zh
-        below = w_all.at[:, pl.ds(pl.multiple_of(first * ROWS_W + CUT_W, 32), ROWS_W - CUT_W)]
+        below = w_all.at[:, pl.ds(pl.multiple_of(first * ROWS_W + CUT_W, 16), ROWS_W - CUT_W)]
         on_z.append(push(below, below, sem_w, 2 * NX + d, at(dz=1)))
 
     halo_wait(f_made, f_got, sem_hf)
@@ -237,10 +249,11 @@
         two = (vf[col, f, 1:17, 1], vf[col, f, 1:17, 0], vf[col, f, 0:16, 0])[b]
         return (one + two).reshape(TOK, FINE).astype(BF)
 
+    scale = gain[...].reshape(1, CH)
     for f, pooled in enumerate(causal(fine_cells, uw, NN)):
-        z = gain[...] * wide(preact[f].reshape(TOK, CH))
+        z = scale * wide(preact[f].reshape(TOK, CH))
         s = 1.0 / (1.0 + jnp.exp(-z))
-        mid = (pooled * gain[...] * s * (1.0 + z * (1.0 - s))).astype(BF)
+        mid = (pooled * scale * s * (1.0 + z * (1.0 - s))).astype(BF)
         mf[f, 1:17, 8:16, :] = wide(mid).reshape(16, 8, CH)
     ms_row[0] = mf[:, 1, 8:16, :]
     ms_row[1] = mf[:, 16, 8:16, :]
@@ -251,8 +264,9 @@
     m_made = [ms_row.at[0], ms_row.at[1], ms_col.at[0], ms_col.at[1]] + [ms_cor.at[i] for i in range(4)]
     m_got = [mr_row.at[0], mr_row.at[1], mr_col.at[0], mr_col.at[1]] + [mr_cor.at[i] for i in range(4)]
     halo_start(m_made, m_got, sem_hm)
-    for copy in local + of_conv[2:]:
-        copy.wait()
+    arrived(kx)
+    start(kz + to_q + vx)
+    of_conv[2].wait()
     halo_wait(m_made, m_got, sem_hm)
     mf[:, 0, 8:16, :] = mr_row[0]
     mf[:, 17, 8:16, :] = mr_row[1]
@@ -281,14 +295,18 @@
     p_all[rows(c, 32), :] = ps[...].astype(BF)
     start(to_p)
 
-    arrived(to_p)
+    arrived(to_p[:1])
+    start(on_p)
+    arrived(to_p[1:] + on_p)
     g_own[...] = mm(p_all[...], pw[...]).astype(BF)
     to_g = to_queries(g_own, g_all, sem_g)
     start(to_g)
+    arrived(vx)
+    start(own_vz + vz + [to_wz, to_w[0], to_w[2]])
     g_all[rows(plane), :] = g_own[:, cols(x)]
     g_all[rows(y, base=FULL), :] = g_own[:, cols(NX)]
 
-    arrived(to_k + to_q)
+    arrived(kz + own_kz + to_q)
 
     def spans(i):
         return rows(i, CHUNK), rows(i // FULL_CHUNKS, KEYS)
@@ -322,7 +340,7 @@
         return 0
 
     lax.fori_loop(0, CHUNKS, share_step, 0)
-    arrived(to_v + to_g)
+    arrived(vz + own_vz + to_g)
 
     def grad_step(i, _):
         span, keys = spans(i)
@@ -362,8 +380,6 @@
     key_sums(probs, g_all, dv_s, dv_r, sem_dv, 1.0)
     to_dv = all_key_copies(dv_s, dv_r, sem_dv)
     arrived(to_rd)
-    arrived(to_w)
-    start(on_x + on_z)
 
     def query_copies(d):
         copies = []
@@ -399,6 +415,10 @@
     dl_r[y] = dq_s[rows(y, base=FULL), :]
     key_sums(gp, q_all, dk_s, dk_r, sem_dk, FACTOR)
     to_dk = all_key_copies(dk_s, dk_r, sem_dk)
+    to_wz.wait_recv()
+    start([to_w[1]] + on_x)
+    arrived([to_w[0], to_w[2]])
+    start([on_z[0], on_z[2]])
     to_dq = [copy for d in range(NY) for copy in query_copies(d)]
 
     def key_total(part_index, got):
@@ -431,6 +451,8 @@
         total = total + wide(dl_r[j])
     a_all[0, rows(y), NX * HEAD_DIM :] = total.astype(BF)
     start(to_a[0])
+    arrived([to_w[1]])
+    start([on_z[1]])
     arrived(to_dk)
     key_total(1, dk_r)
     start(to_a[1])
@@ -489,7 +511,7 @@
             span = pl.ds(half * HALF + first, size)
             out[:, span] = (wide(red[0, :, span]) + wide(red[1, :, span])).astype(BF)
 
-    done = to_p + to_k + to_q + to_v + to_w + on_x + on_z + to_g + to_st + to_rd + to_dv + to_dq + to_dl + to_dk
+    done = to_p + on_p + [to_wz] + to_k + to_q + to_v + to_w + on_x + on_z + to_g + to_st + to_rd + to_dv + to_dq + to_dl + to_dk
     for copy in done + to_a[0] + to_a[1] + to_a[2] + to_c:
         copy.wait_send()
     halo_wait(f_made, f_got, sem_hf, sent=True)
@@ -604,7 +626,7 @@
     )(
         out_grad.reshape(2, 16, 2, 16, FINE),
         preact,
-        norm_gain.reshape(1, CH),
+        norm_gain,
         up_weight.transpose(0, 1, 2, 4, 3).reshape(3, 9, FINE, CH),
         mid_weight.reshape(3, 9, CH, CH),
         patch_weight,

time: 157 us -> 120 us (0.76); the launches traced: 155 us -> 120 us
  Pallas kernels: 150 us -> 116 us
    pallas_call x1, Pallas kernels: 150 us -> 116 us  [body(): pl.pallas_call(whole_kernel, out_shape=(jax.ShapeDtypeStruct((2, 16, 8, C...]
where the time goes in v5:
time: 120 us
  Pallas kernels  116 us (97%)
  local copies, waits for them, and re-layouts  3.34 us (3%)
    pallas_call x1, Pallas kernels, body(): pl.pallas_call(whole_kernel, out_shape=(jax.ShapeDtypeStruct((2, 16, 8, C...  116 us
    unnamed x2, local copies, waits for them, and re-layouts  3.34 us

profile of v5, /device:TPU:1, one launch (start us, length us, event | category | flops | bytes accessed | tf_op | source)
XLA Modules:
  0.0 120.0 jit_solution(13621281982681266902)
XLA Ops:
  0.6 116.0 %whole.1 = (bf16[2,16,8,384]{3,2,1,0:T(8,128)(2,1)}, bf16[128,1280]{1,0:T(8,128)(2,1)}) custom-call(bf16[2,16,2,16,192]{4,3,2,1,0:T(8,128)(2,1)} %bitcast.9, bf16[2,16,8,384]{3,2,1,0:T(8,128)(2,1)} %preact.1, f32[384]{0:T(512)} %gain.1, bf16[3,9,192,384]{3,2,1,0:T(8,128)(2,1)} %bitcast.7, bf16[3,9,384,384]{3,2,1,0:T(8,128)(2,1)} %bitcast.6, ...), custom_call_target="tpu_custom_call" | custom-call | tf_op jit(solution)/shard_map/whole/pallas_call | solution.py:550
  116.6 1.6 %copy.14 = bf16[2,16,8,384]{3,2,1,0:T(8,128)(2,1)} copy(bf16[2,16,8,384]{3,2,1,0:T(8,128)(2,1)} %get-tuple-element.4) | data formatting | bytes 393216
  118.3 1.7 %copy.15 = bf16[128,1280]{1,0:T(8,128)(2,1)} copy(bf16[128,1280]{1,0:T(8,128)(2,1)} %get-tuple-element.5) | data formatting | bytes 655360

commit v6 on v5

--- a/solution.py
+++ b/solution.py
@@ -27,7 +27,8 @@
 FULL_CHUNKS = FULL // CHUNK
 CHUNKS = QUERIES // CHUNK
 ROWS_W = 160
-CUT_W = 48
+CUT_W = 64
+EARLY_W = 64
 OUT = NK * ROWS_W
 HALF = OUT // 2
 PIECES = ((0, 256), (256, 256), (512, 128))
@@ -129,25 +130,27 @@
 
     plane = y * NX + x
     line = x * NZ + zh
-    local = [
-        pltpu.make_async_copy(patch_w, pw, sem_l.at[1]),
-        pltpu.make_async_copy(query.at[:, cols(x)], q_all.at[rows(plane)], sem_l.at[2]),
-        pltpu.make_async_copy(query.at[:, cols(NX)], q_all.at[rows(y, base=FULL)], sem_l.at[3]),
-        pltpu.make_async_copy(key.at[:, cols(x)], k_all.at[rows(line)], sem_l.at[4]),
-        pltpu.make_async_copy(key.at[:, cols(NX)], k_all.at[rows(line, base=KEYS)], sem_l.at[5]),
-        pltpu.make_async_copy(value.at[:, cols(x)], v_all.at[rows(line)], sem_l.at[6]),
-        pltpu.make_async_copy(value.at[:, cols(NX)], v_all.at[rows(line, base=KEYS)], sem_l.at[7]),
-        pltpu.make_async_copy(weight, w_all.at[:, rows(line, ROWS_W)], sem_l.at[8]),
+    def load(src, dst, index):
+        return pltpu.make_async_copy(src, dst, sem_l.at[index])
+
+    in_fine = load(fine, g_in, 0)
+    in_up = load(up_w.at[pl.ds(1, 2)], uw, 1)
+    in_mid = load(mid_w.at[pl.ds(1, 2)], mw, 2)
+    in_patch = load(patch_w, pw, 3)
+    in_weight = load(weight, w_all.at[:, rows(line, ROWS_W)], 4)
+    in_key = [
+        load(key.at[:, cols(x)], k_all.at[rows(line)], 5),
+        load(key.at[:, cols(NX)], k_all.at[rows(line, base=KEYS)], 6),
     ]
-    of_conv = [
-        pltpu.make_async_copy(fine, g_in, sem_l.at[0]),
-        pltpu.make_async_copy(up_w.at[pl.ds(1, 2)], uw, sem_l.at[9]),
-        pltpu.make_async_copy(mid_w.at[pl.ds(1, 2)], mw, sem_l.at[10]),
+    in_rest = [
+        load(value.at[:, cols(x)], v_all.at[rows(line)], 7),
+        load(value.at[:, cols(NX)], v_all.at[rows(line, base=KEYS)], 8),
+        load(query.at[:, cols(x)], q_all.at[rows(plane)], 9),
+        load(query.at[:, cols(NX)], q_all.at[rows(y, base=FULL)], 10),
     ]
-    start(of_conv)
-    start(local)
-
-    of_conv[0].wait()
+    start([in_fine] + in_key + [in_up] + in_rest + [in_mid, in_patch, in_weight])
+
+    in_fine.wait()
     lanes = ((0, 0, HEAD_DIM), (1, HEAD_DIM, FINE - HEAD_DIM))
     for k, first, size in lanes:
         span = slice(first, first + size)
@@ -203,12 +206,22 @@
     own_kz, own_vz = keys_over_z(k_all, sem_k, (0,)), keys_over_z(v_all, sem_v, (0,))
     to_k, to_v = kx + kz + own_kz, vx + vz + own_vz
     to_q = to_queries(query, q_all, sem_q)
-    mine = w_all.at[:, rows(line, ROWS_W)]
-    to_w = [push(weight, mine, sem_w, d, at(dx=d)) for d in range(1, NX)]
-    to_wz = push(weight, mine, sem_w, 0, at(dz=1))
-    for copy in local:
+
+    def some_rows(d, first, size, slot):
+        mine = w_all.at[:, pl.ds(pl.multiple_of(line * ROWS_W + first, 16), size)]
+        return push(weight.at[:, pl.ds(first, size)], mine, sem_w, slot + d, at(dx=d))
+
+    wx = [
+        [some_rows(d, 0, EARLY_W, 0) for d in range(1, NX)],
+        [some_rows(d, EARLY_W, ROWS_W - EARLY_W, 3 * NX) for d in range(1, NX)],
+    ]
+    wz = [
+        push(weight.at[:, pl.ds(first, size)], w_all.at[:, pl.ds(pl.multiple_of(line * ROWS_W + first, 16), size)], sem_w, slot, at(dz=1))
+        for first, size, slot in ((0, CUT_W, 0), (CUT_W, ROWS_W - CUT_W, 3 * NX))
+    ]
+    for copy in in_key:
         copy.wait()
-    start(kx + own_kz)
+    start(kx + own_kz + wz[:1])
     beside = w_all.at[:, pl.ds(pl.multiple_of((x * NZ + 1 - zh) * ROWS_W, 16), CUT_W)]
     on_x = [push(beside, beside, sem_w, NX + d, at(dx=d)) for d in range(1, NX)]
     on_z = []
@@ -231,7 +244,7 @@
             four = [gf[k, f, :, :, pl.ds(7 + s, 8, stride=2), :][..., :size] for s in range(4)]
             for tap in range(3):
                 vf[tap, f, :, :, :, span] = four[2 - tap] + four[3 - tap]
-    of_conv[1].wait()
+    in_up.wait()
 
     def causal(cells, weights, dims):
         own = later = None
@@ -265,8 +278,8 @@
     m_got = [mr_row.at[0], mr_row.at[1], mr_col.at[0], mr_col.at[1]] + [mr_cor.at[i] for i in range(4)]
     halo_start(m_made, m_got, sem_hm)
     arrived(kx)
-    start(kz + to_q + vx)
-    of_conv[2].wait()
+    start(kz + to_q + vx + [wx[0][0], wx[0][2]])
+    in_mid.wait()
     halo_wait(m_made, m_got, sem_hm)
     mf[:, 0, 8:16, :] = mr_row[0]
     mf[:, 17, 8:16, :] = mr_row[1]
@@ -297,12 +310,15 @@
 
     arrived(to_p[:1])
     start(on_p)
+    for copy in in_rest + [in_patch, in_weight]:
+        copy.wait()
+    arrived(vx)
+    start(own_vz + vz + wz[1:])
     arrived(to_p[1:] + on_p)
     g_own[...] = mm(p_all[...], pw[...]).astype(BF)
     to_g = to_queries(g_own, g_all, sem_g)
     start(to_g)
-    arrived(vx)
-    start(own_vz + vz + [to_wz, to_w[0], to_w[2]])
+    start([wx[1][0], wx[1][2]])
     g_all[rows(plane), :] = g_own[:, cols(x)]
     g_all[rows(y, base=FULL), :] = g_own[:, cols(NX)]
 
@@ -321,7 +337,7 @@
         probs[:, span] = e.astype(BF)
         return 0
 
-    lax.fori_loop(0, CHUNKS, score_step, 0)
+    lax.fori_loop(0, CHUNKS, score_step, 0, unroll=2)
     to_st = [push(stat_s, stat_r.at[y], sem_st, d, at(dy=d)) for d in range(1, NY)]
     start(to_st)
     stat_r[y] = stat_s[...]
@@ -339,7 +355,7 @@
         probs[:, span] = (wide(probs[:, span]) * share).astype(BF)
         return 0
 
-    lax.fori_loop(0, CHUNKS, share_step, 0)
+    lax.fori_loop(0, CHUNKS, share_step, 0, unroll=2)
     arrived(vz + own_vz + to_g)
 
     def grad_step(i, _):
@@ -349,7 +365,7 @@
         gp[:, span] = g.astype(BF)
         return 0
 
-    lax.fori_loop(0, CHUNKS, grad_step, 0)
+    lax.fori_loop(0, CHUNKS, grad_step, 0, unroll=2)
     to_rd = [push(dot_s, dot_r.at[y], sem_rd, d, at(dy=d)) for d in range(1, NY)]
     start(to_rd)
     dot_r[y] = dot_s[...]
@@ -406,19 +422,19 @@
 
     for d in (2, 1, 3, 0):
         first = lax.rem(y + d, NY) * 2
-        lax.fori_loop(first, first + 2, query_step, 0)
+        query_step(first, 0)
+        query_step(first + 1, 0)
         start(query_copies(d))
-    lax.fori_loop(FULL_CHUNKS, CHUNKS, query_step, 0)
+    query_step(FULL_CHUNKS, 0)
+    query_step(FULL_CHUNKS + 1, 0)
     to_dl = [last_copy(d) for d in range(1, NY)]
     start(to_dl)
     dq_r[plane] = dq_s[rows(plane), :]
     dl_r[y] = dq_s[rows(y, base=FULL), :]
     key_sums(gp, q_all, dk_s, dk_r, sem_dk, FACTOR)
     to_dk = all_key_copies(dk_s, dk_r, sem_dk)
-    to_wz.wait_recv()
-    start([to_w[1]] + on_x)
-    arrived([to_w[0], to_w[2]])
-    start([on_z[0], on_z[2]])
+    arrived(wz[:1])
+    start([wx[0][1], wx[1][1]] + on_x)
     to_dq = [copy for d in range(NY) for copy in query_copies(d)]
 
     def key_total(part_index, got):
@@ -434,12 +450,21 @@
 
     def a_copies(k):
         mine = a_all.at[k, rows(y)]
-        return [push(mine, mine, sem_a, k * NY + d, at(dy=d)) for d in range(1, NY)]
+        return [push(mine, mine, sem_a, k * NY + d, at(dy=d)) for d in (1, 3)]
+
+    def a_onward(k):
+        half = TOK // 2
+        up = a_all.at[k, pl.ds(pl.multiple_of(lax.rem(y + 3, NY) * TOK, half), half)]
+        down = a_all.at[k, pl.ds(pl.multiple_of(lax.rem(y + 1, NY) * TOK + half, half), half)]
+        return [push(up, up, sem_a, k * NY, at(dy=1)), push(down, down, sem_a, k * NY + 2, at(dy=3))]
 
     to_a = [a_copies(k) for k in range(3)]
+    on_a = [a_onward(k) for k in range(3)]
     arrived(to_dv)
     key_total(2, dv_r)
     start(to_a[2])
+    arrived([wx[0][0], wx[0][2], wx[1][0], wx[1][2]])
+    start([on_z[0], on_z[2]])
     arrived(to_dq + to_dl)
     for h in range(NX):
         total = wide(dq_r[h])
@@ -451,14 +476,20 @@
         total = total + wide(dl_r[j])
     a_all[0, rows(y), NX * HEAD_DIM :] = total.astype(BF)
     start(to_a[0])
-    arrived([to_w[1]])
+    arrived(to_a[2])
+    start(on_a[2])
+    arrived([wx[0][1], wx[1][1]])
     start([on_z[1]])
     arrived(to_dk)
     key_total(1, dk_r)
     start(to_a[1])
-    arrived(on_x + on_z)
+    arrived(to_a[0])
+    start(on_a[0])
+    arrived(to_a[1])
+    start(on_a[1])
     for k in (2, 0, 1):
-        arrived(to_a[k])
+        arrived(on_a[k])
+    arrived(wz[1:] + on_x + on_z)
 
     def project(first, size):
         span = pl.ds(pl.multiple_of(first, HEAD_DIM), size)
@@ -498,6 +529,12 @@
         @pl.when(c != y)
         def _():
             out_copy(n, 0).start()
+
+    done = to_p + on_p + wz + to_k + to_q + to_v + wx[0] + wx[1] + on_x + on_z + to_g + to_st + to_rd + to_dv + to_dq + to_dl + to_dk
+    for copy in done + to_a[0] + to_a[1] + to_a[2] + on_a[0] + on_a[1] + on_a[2] + to_c:
+        copy.wait_send()
+    halo_wait(f_made, f_got, sem_hf, sent=True)
+    halo_wait(m_made, m_got, sem_hm, sent=True)
 
     for n, (first, size) in enumerate(PIECES):
         for other in range(TY):
@@ -511,11 +548,6 @@
             span = pl.ds(half * HALF + first, size)
             out[:, span] = (wide(red[0, :, span]) + wide(red[1, :, span])).astype(BF)
 
-    done = to_p + on_p + [to_wz] + to_k + to_q + to_v + to_w + on_x + on_z + to_g + to_st + to_rd + to_dv + to_dq + to_dl + to_dk
-    for copy in done + to_a[0] + to_a[1] + to_a[2] + to_c:
-        copy.wait_send()
-    halo_wait(f_made, f_got, sem_hf, sent=True)
-    halo_wait(m_made, m_got, sem_hm, sent=True)
     for n in range(len(PIECES)):
         for d in range(1, NY):
             out_copy(n, d).wait_send()
@@ -607,7 +639,7 @@
             sems(NY * NX + NY),
             sems(2 * NK),
             sems(2 * NK),
-            sems(3 * NX),
+            sems(4 * NX),
             sems(NY * NX + NY),
             sems(NY),
             sems(NY),

time: 120 us -> 117 us (0.975)
  Pallas kernels: 116 us -> 113 us
    pallas_call x1, Pallas kernels: 116 us -> 113 us  [body(): pl.pallas_call(whole_kernel, out_shape=(jax.ShapeDtypeStruct((2, 16, 8, C...]
where the time goes in v6:
time: 117 us
  Pallas kernels  113 us (97%)
  local copies, waits for them, and re-layouts  3.34 us (3%)
    pallas_call x1, Pallas kernels, body(): pl.pallas_call(whole_kernel, out_shape=(jax.ShapeDtypeStruct((2, 16, 8, C...  113 us
    unnamed x2, local copies, waits for them, and re-layouts  3.34 us

profile of v6, /device:TPU:1, one launch (start us, length us, event | category | flops | bytes accessed | tf_op | source)
XLA Modules:
  0.0 116.8 jit_solution(12734181558118594362)
XLA Ops:
  0.6 112.8 %whole.1 = (bf16[2,16,8,384]{3,2,1,0:T(8,128)(2,1)}, bf16[128,1280]{1,0:T(8,128)(2,1)}) custom-call(bf16[2,16,2,16,192]{4,3,2,1,0:T(8,128)(2,1)} %bitcast.9, bf16[2,16,8,384]{3,2,1,0:T(8,128)(2,1)} %preact.1, f32[384]{0:T(512)} %gain.1, bf16[3,9,192,384]{3,2,1,0:T(8,128)(2,1)} %bitcast.7, bf16[3,9,384,384]{3,2,1,0:T(8,128)(2,1)} %bitcast.6, ...), custom_call_target="tpu_custom_call" | custom-call | tf_op jit(solution)/shard_map/whole/pallas_call | solution.py:582
  113.4 1.6 %copy.14 = bf16[2,16,8,384]{3,2,1,0:T(8,128)(2,1)} copy(bf16[2,16,8,384]{3,2,1,0:T(8,128)(2,1)} %get-tuple-element.4) | data formatting | bytes 393216
  115.1 1.7 %copy.15 = bf16[128,1280]{1,0:T(8,128)(2,1)} copy(bf16[128,1280]{1,0:T(8,128)(2,1)} %get-tuple-element.5) | data formatting | bytes 655360

commit v7 on v6

--- a/solution.py
+++ b/solution.py
@@ -498,7 +498,8 @@
         return total + mm(a_all[2], w_all[2, span, :], NT)
 
     to_c = []
-    for n, (first, size) in enumerate(PIECES):
+    def give(n):
+        first, size = PIECES[n]
         part[:, first : first + size] = project((1 - core) * HALF + first, size).astype(BF)
         span = pl.ds(first, size)
         copy = push(part.at[:, span], pair.at[:, span], sem_c, n, partner)
@@ -514,7 +515,8 @@
             (y // 2, lax.rem(y, 2), to, x, zh), n * NY + c,
         )
 
-    for n, (first, size) in enumerate(PIECES):
+    def keep(n):
+        first, size = PIECES[n]
         total = project(core * HALF + first, size)
         to_c[n].wait_recv()
         span = pl.ds(first, size)
@@ -529,6 +531,13 @@
         @pl.when(c != y)
         def _():
             out_copy(n, 0).start()
+
+    give(0)
+    give(1)
+    keep(0)
+    give(2)
+    keep(1)
+    keep(2)
 
     done = to_p + on_p + wz + to_k + to_q + to_v + wx[0] + wx[1] + on_x + on_z + to_g + to_st + to_rd + to_dv + to_dq + to_dl + to_dk
     for copy in done + to_a[0] + to_a[1] + to_a[2] + on_a[0] + on_a[1] + on_a[2] + to_c:

time: 117 us -> 117 us (level)
  no operation moved by 1% of the time
where the time goes in v7:
time: 117 us; the launch traced here: 116 us
  Pallas kernels  112 us (96%)
  local copies, waits for them, and re-layouts  3.34 us (3%)
    pallas_call x1, Pallas kernels, body(): pl.pallas_call(whole_kernel, out_shape=(jax.ShapeDtypeStruct((2, 16, 8, C...  112 us
    unnamed x2, local copies, waits for them, and re-layouts  3.34 us

profile of v7, /device:TPU:1, one launch (start us, length us, event | category | flops | bytes accessed | tf_op | source)
XLA Modules:
  0.0 116.0 jit_solution(12975297144642047088)
XLA Ops:
  0.6 112.0 %whole.1 = (bf16[2,16,8,384]{3,2,1,0:T(8,128)(2,1)}, bf16[128,1280]{1,0:T(8,128)(2,1)}) custom-call(bf16[2,16,2,16,192]{4,3,2,1,0:T(8,128)(2,1)} %bitcast.9, bf16[2,16,8,384]{3,2,1,0:T(8,128)(2,1)} %preact.1, f32[384]{0:T(512)} %gain.1, bf16[3,9,192,384]{3,2,1,0:T(8,128)(2,1)} %bitcast.7, bf16[3,9,384,384]{3,2,1,0:T(8,128)(2,1)} %bitcast.6, ...), custom_call_target="tpu_custom_call" | custom-call | tf_op jit(solution)/shard_map/whole/pallas_call | solution.py:591
  112.6 1.6 %copy.14 = bf16[2,16,8,384]{3,2,1,0:T(8,128)(2,1)} copy(bf16[2,16,8,384]{3,2,1,0:T(8,128)(2,1)} %get-tuple-element.4) | data formatting | bytes 393216
  114.3 1.7 %copy.15 = bf16[128,1280]{1,0:T(8,128)(2,1)} copy(bf16[128,1280]{1,0:T(8,128)(2,1)} %get-tuple-element.5) | data formatting | bytes 655360
